TPU v7x, 128 devices: a whole 4x4x4 slice. The times are simulated.
128 devices in a mesh: dev: 128 (over y, z, x, core).
Axes of the slice: x: 4, y: 4, z: 4, core: 2. Of those that a mesh axis runs over, the one named last changes fastest.
Arguments:
- dynamics: float32 [2, 72, 65536], P(None, None, 'dev'), may hold values from -6 to 6
- adjacency: int32 [2, 16384], P(None, 'dev'), may hold values from 0 to 4095, as said below
- cloud_state: float32 [2, 58, 64, 16384], P(None, None, None, 'dev'), may hold values from -6 to 6
- span_source: int32 [16384], P('dev'), may hold values from 0 to 16383, as said below
- substeps: int32 [1024], P('dev'), may hold values from 1 to 12
Outputs:
- dynamics_summed: float32 [2, 72, 65536], P(None, None, 'dev')
- tendency: float32 [2, 58, 16384], P(None, None, 'dev')
- cloud_new: float32 [2, 58, 64, 16384], P(None, None, None, 'dev')
Inputs may be any that keep to these rules, and one draw needn't show every extreme that they name: `adjacency`: edges match in pairs: edge k of e faces edge m of f exactly when edge m of f faces edge k of e. The element across an edge belongs to the same block of 32 elements or to the block just below or above, cyclically. `span_source`: A permutation of the columns. Each block of 128 slots holds exactly 1 column of each block of 128 columns.
All inputs are finite; a program needn't handle non-finite values.
Results may differ from a plain program's by a relative error of at most 0.0003.
Values sent between devices are 32-bit elements; how exact they have to be, the bound alone decides.
A program may use at most 128 MiB of HBM per device.

v0:
```python
import jax
import jax.numpy as jnp
import numpy as np
from jax import lax
from jax.sharding import PartitionSpec as P

edge_nodes = ((1, 2), (7, 11), (14, 13), (8, 4))
relax_rate = 0.3
diffusion = 0.1
latent_heat = 1.0


def padded_2(x, sides, width):
    for axis, dim in sides:
        size, length = (lax.axis_size(axis), x.shape[dim])
        up = [(i, (i + 1) % size) for i in range(size)]
        down = [(j, i) for i, j in up]
        last = lax.slice_in_dim(x, length - width, length, axis=dim)
        leading = lax.slice_in_dim(x, 0, width, axis=dim)
        before = lax.ppermute(last, axis, up)
        after = lax.ppermute(leading, axis, down)
        x = jnp.concatenate([before, x, after], axis=dim)
    return x


def node_slot_table():
    table = np.full((16,), -1, np.int32)
    for edge in range(4):
        for which in range(2):
            table[edge_nodes[edge][which]] = edge * 2 + which
    return table


def pooling_table(node_count):
    node = np.arange(node_count)
    inner = node % 16
    target = 4 * (node // 16) + 2 * (inner // 4 // 2) + inner % 4 // 2
    table = np.zeros((node_count, node_count // 4), np.float32)
    table[node, target] = 0.25
    return jnp.asarray(table)


def cloud_step(state, forcing, counts, trip_count):
    fields, depth, width, group = state.shape
    heights = jnp.arange(depth).astype(jnp.float32)
    saturation = (0.8 * jnp.exp(-2.0 * heights / depth))[:, None]
    start_mean = jnp.mean(state, axis=2)
    flat = state.reshape(fields, depth, width * group)
    live = jnp.tile(counts, width)

    def across(values):
        return jnp.mean(values.reshape(fields, depth, width, group), axis=2)

    def substep(step_index, current):
        average = across(current)
        relaxed = current + relax_rate * jnp.tile(forcing - average, (1, 1, width))
        above = jnp.concatenate([relaxed[:, 1:], relaxed[:, -1:]], axis=1)
        below = jnp.concatenate([relaxed[:, :1], relaxed[:, :-1]], axis=1)
        laplace = (
            jnp.roll(relaxed, group, axis=2)
            + jnp.roll(relaxed, -group, axis=2)
            + above
            + below
            - 4.0 * relaxed
        )
        diffused = relaxed + diffusion * laplace
        condensed = 0.5 * jnp.maximum(diffused[1] - saturation - 0.5 * diffused[0], 0.0)
        stepped = jnp.stack([diffused[0] + latent_heat * condensed, diffused[1] - condensed])
        active = (step_index < live)[None, None, :]
        return jnp.where(active, stepped, current)

    final = lax.fori_loop(0, trip_count, substep, flat).reshape(fields, depth, width, group)
    return (final, jnp.mean(final, axis=2) - start_mean)


def run_blocks(state, forcing, counts, span_size):
    new_parts = []
    tend_parts = []
    for block in range(state.shape[3] // span_size):
        lower = block * span_size
        block_counts = counts[lower : lower + span_size]
        final, tend = cloud_step(
            state[..., lower : lower + span_size],
            forcing[..., lower : lower + span_size],
            block_counts,
            jnp.max(block_counts),
        )
        new_parts.append(final)
        tend_parts.append(tend)
    return (jnp.concatenate(new_parts, axis=3), jnp.concatenate(tend_parts, axis=2))


def on_device(dynamics, adjacency, cloud_state, span_source, substeps):
    devices = lax.axis_size("dev")
    position = lax.axis_index("dev")
    fields, levels, node_count = dynamics.shape
    elements = node_count // 16
    element_of = jnp.arange(node_count, dtype=jnp.int32) // 16
    edge_flat = (
        jnp.arange(elements, dtype=jnp.int32)[:, None] * 16
        + jnp.array(edge_nodes, jnp.int32).reshape(1, 8)
    ).reshape(-1)
    edge_values = dynamics[..., edge_flat]
    padded = padded_2(edge_values, (("dev", 2),), elements * 8)
    neighbour = adjacency[0]
    facing = adjacency[1]
    offset_rank = (neighbour // elements - position + 1) % devices
    placed = offset_rank * elements + neighbour % elements
    base_partner = placed * 8 + facing * 2
    slot_table = jnp.asarray(node_slot_table())
    node_slot = jnp.tile(slot_table, elements)
    on_edge = node_slot >= 0
    safe_slot = jnp.maximum(node_slot, 0)
    edge_of_node = element_of * 4 + safe_slot // 2
    partner = base_partner[edge_of_node] + 1 - safe_slot % 2
    opposite = padded[..., partner]
    dynamics_summed = jnp.where(on_edge[None, None, :], 0.5 * (dynamics + opposite), dynamics)
    depth = cloud_state.shape[1]
    lower_levels = dynamics_summed[:, :depth].reshape(fields * depth, node_count)
    forcing = jnp.dot(
        lower_levels,
        pooling_table(node_count),
        precision=lax.Precision.HIGHEST,
        preferred_element_type=jnp.float32,
    ).reshape(fields, depth, node_count // 4)
    columns = forcing.shape[2]
    per_peer = columns // devices
    span_size = columns // substeps.shape[0]
    slot_counts = jnp.repeat(substeps, span_size)
    owner_rank = span_source // columns
    sorted_slots = jnp.argsort(owner_rank, stable=True)
    inverse_slots = jnp.argsort(sorted_slots)
    wanted = (span_source[sorted_slots] % columns).reshape(devices, per_peer)
    asked = lax.all_to_all(wanted, "dev", split_axis=0, concat_axis=0, tiled=True)
    asked_flat = asked.reshape(-1)
    inverse_asked = jnp.argsort(asked_flat)
    send_state = cloud_state[..., asked_flat]
    send_force = forcing[..., asked_flat][:, :, None, :]
    got_state, got_force = (
        lax.all_to_all(send_state, "dev", split_axis=3, concat_axis=3, tiled=True),
        lax.all_to_all(send_force, "dev", split_axis=3, concat_axis=3, tiled=True),
    )
    slot_state = got_state[..., inverse_slots]
    slot_force = got_force[:, :, 0, inverse_slots]
    new_slots, tend_slots = run_blocks(slot_state, slot_force, slot_counts, span_size)
    back_state = new_slots[..., sorted_slots]
    back_tend = tend_slots[..., sorted_slots][:, :, None, :]
    ret_state, ret_tend = (
        lax.all_to_all(back_state, "dev", split_axis=3, concat_axis=3, tiled=True),
        lax.all_to_all(back_tend, "dev", split_axis=3, concat_axis=3, tiled=True),
    )
    cloud_new = ret_state[..., inverse_asked]
    tendency = ret_tend[:, :, 0, inverse_asked]
    return (dynamics_summed, tendency, cloud_new)


def solution(mesh):
    in_specs = (
        P(None, None, "dev"),
        P(None, "dev"),
        P(None, None, None, "dev"),
        P("dev"),
        P("dev"),
    )
    out_specs = (P(None, None, "dev"), P(None, None, "dev"), P(None, None, None, "dev"))
    return jax.shard_map(
        on_device, mesh=mesh, in_specs=in_specs, out_specs=out_specs, check_vma=False
    )
```

profile of v0, /device:TPU:0, one launch (start us, length us, event | category | flops | bytes accessed | tf_op | source)
XLA Modules:
  0.0 509.7 jit_solution(5820993389495066980)
XLA Ops:
  3.7 8.3 %collective-permute-start.1 = (f32[2,72,256]{1,0,2:T(2,128)S(1)}, f32[2,72,256]{1,0,2:T(2,128)S(1)}, u32[]{:S(2)}, u32[]{:S(2)}) collective-permute-start(f32[2,72,256]{1,0,2:T(2,128)S(1)} %bitcast.212), channel_id=1, source_target_pairs={{1,0},{2,1},{3,2},{4,3},{5,4},{6,5},{7,6},{8,7},{9,8},{10,9},{11,1... | collective-permute-start | bytes 442376 | tf_op jit(solution)/shard_map/ppermute | solution.py:21
  12.6 2.5 sort.48
  15.2 1.6 gather_fusion.3
  17.5 9.1 %all-to-all-start = ((s32[128,1,1]{2,1,0:T(1,128)}), s32[128,1,1]{2,1,0:T(1,128)S(1)}, u32[]{:S(2)}, u32[]{:S(2)}) async-start(s32[128,1,1]{2,1,0:T(1,128)} %copy.693), calls=%async_computation | async-start | bytes 131072 | tf_op jit(solution)/shard_map/all_to_all | solution.py:134
  30.4 5.4 %all-to-all-done = s32[128,1,1]{2,1,0:T(1,128)S(1)} async-done(((s32[128,1,1]{2,1,0:T(1,128)}), s32[128,1,1]{2,1,0:T(1,128)S(1)}, u32[]{:S(2)}, u32[]{:S(2)}) %all-to-all-start) | async-done | bytes 544 | tf_op jit(solution)/shard_map/all_to_all | solution.py:134
  35.9 2.3 reduce
  38.2 3.3 gather_fusion.1
  42.1 2.1 gather_fusion.2
  48.9 5.0 all-to-all-start.2
  53.9 9.0 %copy.694 = f32[2,58,64,128]{2,1,0,3:T(8,128)} copy(f32[2,58,64,128]{3,2,1,0:T(8,128)} %param.26) | data formatting | bytes 7602176 | tf_op args[2]
  62.9 7.7 %gather_fusion.4 = f32[128,2,58,64]{3,2,1,0:T(8,128)} fusion(f32[2,58,64,128]{2,1,0,3:T(8,128)} %copy.694, s32[1024]{0:T(1024)S(1)} %get-tuple-element.1065), kind=kCustom, calls=%fused_computation.4 | custom fusion | bytes 7602688 | tf_op jit(solution)/shard_map/gather | solution.py:137
  70.6 13.9 %copy.782 = f32[2,58,64,128]{2,0,1,3:T(2,128)} copy(f32[2,58,64,128]{2,1,0,3:T(8,128)} %bitcast.210) | data formatting | bytes 7602176 | tf_op jit(solution)/shard_map/gather | solution.py:137
  84.5 10.2 %reshape.766 = f32[128,1,7424]{2,1,0:T(1,128)} reshape(f32[128,58,2,64]{3,2,1,0:T(2,128)} %bitcast.204) | data formatting | bytes 7602176
  94.7 10.3 %all-to-all-start.1 = ((f32[128,1,7424]{2,1,0:T(1,128)}), f32[128,1,7424]{2,1,0:T(1,128)}, u32[]{:S(2)}, u32[]{:S(2)}) async-start(f32[128,1,7424]{2,1,0:T(1,128)} %reshape.766), calls=%async_computation.1 | async-start | bytes 7602176 | tf_op jit(solution)/shard_map/all_to_all | solution.py:140
  105.0 2.5 sort.49
  108.3 2.5 sort.50
  115.7 37.6 %all-to-all-done.1 = f32[128,1,7424]{2,1,0:T(1,128)} async-done(((f32[128,1,7424]{2,1,0:T(1,128)}), f32[128,1,7424]{2,1,0:T(1,128)}, u32[]{:S(2)}, u32[]{:S(2)}) %all-to-all-start.1) | async-done | bytes 3801120 | tf_op jit(solution)/shard_map/all_to_all | solution.py:140
  153.9 13.1 %reduce.2 = f32[128,7424]{1,0:T(8,128)} reduce(f32[128,1,7424]{2,1,0:T(1,128)} %all-to-all-done.1, f32[]{:T(128)} %broadcast.1129), dimensions={1}, to_apply=%all_to_all.20.reduce_sub_computation | reduce | bytes 7602180 | tf_op jit(solution)/shard_map/all_to_all | solution.py:140
  167.0 8.6 %reshape.767 = f32[128,58,2,64]{3,2,1,0:T(2,128)} reshape(f32[128,7424]{1,0:T(8,128)} %reduce.2) | data formatting | bytes 7602176
  175.6 7.6 %copy.696 = f32[2,58,64,128]{2,1,0,3:T(8,128)} copy(f32[2,58,64,128]{2,0,1,3:T(2,128)} %bitcast.205) | data formatting | bytes 7602176 | tf_op jit(solution)/shard_map/all_to_all | solution.py:140
  183.3 7.7 %gather_fusion.5 = f32[128,2,58,64]{3,2,1,0:T(8,128)} fusion(f32[2,58,64,128]{2,1,0,3:T(8,128)} %copy.696, s32[1024]{0:T(1024)S(1)} %get-tuple-element.1064), kind=kCustom, calls=%fused_computation.5 | custom fusion | bytes 7602688 | tf_op jit(solution)/shard_map/gather | solution.py:143
  190.9 8.0 %slice_reduce_fusion = (f32[2,58,16]{1,0,2:T(2,128)}, f32[2,58,16]{1,0,2:T(2,128)}, f32[2,58,16]{1,0,2:T(2,128)}, f32[2,58,16]{1,0,2:T(2,128)}, f32[2,58,16]{1,0...) fusion(f32[2,58,64,128]{2,1,0,3:T(8,128)} %bitcast.209), kind=kLoop, calls=%fused_computation.220 | loop fusion | flops 935424 | bytes 7661568 | tf_op jit(solution)/shard_map/reduce_sum | solution.py:47
  199.5 6.1 %while.103 = (s32[]{:T(128)}, f32[2,58,1024]{1,2,0:T(8,128)S(1)}, s32[]{:T(128)}, f32[2,58,16]{1,2,0:T(8,128)S(1)}, s32[]{:T(128)}, /*index=5*/f32[]{:T(128)}) while((s32[]{:T(128)}, f32[2,58,1024]{1,2,0:T(8,128)S(1)}, s32[]{:T(128)}, f32[2,58,16]{1,2,0:T(8,128)S(1)}, s32[]{:T(128)}, /*index=5*/f32[]{:T(128)}) %tuple.433), condition=%wide.region_39.40_spmd.clone.clone, body=%wide.region_37.39_spmd.clone.clone.sunk | while | flops 2201393 | bytes 13341483 | solution.py:72
  207.8 1.8 copy.718
  209.6 11.1 %while.102 = (s32[]{:T(128)}, f32[2,58,1024]{1,2,0:T(8,128)S(1)}, s32[]{:T(128)}, f32[2,58,16]{1,2,0:T(8,128)S(1)}, s32[]{:T(128)}, /*index=5*/f32[]{:T(128)}) while((s32[]{:T(128)}, f32[2,58,1024]{1,2,0:T(8,128)S(1)}, s32[]{:T(128)}, f32[2,58,16]{1,2,0:T(8,128)S(1)}, s32[]{:T(128)}, /*index=5*/f32[]{:T(128)}) %tuple.434), condition=%wide.region_34.35_spmd.clone.clone, body=%wide.region_32.34_spmd.clone.clone.sunk | while | flops 2201393 | bytes 13341483 | solution.py:72
  221.4 1.6 copy.733
  222.9 1.8 copy.715
  224.7 10.4 %while.101 = (s32[]{:T(128)}, f32[2,58,1024]{1,2,0:T(8,128)S(1)}, s32[]{:T(128)}, f32[2,58,16]{1,2,0:T(8,128)S(1)}, s32[]{:T(128)}, /*index=5*/f32[]{:T(128)}) while((s32[]{:T(128)}, f32[2,58,1024]{1,2,0:T(8,128)S(1)}, s32[]{:T(128)}, f32[2,58,16]{1,2,0:T(8,128)S(1)}, s32[]{:T(128)}, /*index=5*/f32[]{:T(128)}) %tuple.435), condition=%wide.region_29.30_spmd.clone.clone, body=%wide.region_27.29_spmd.clone.clone.sunk | while | flops 2201393 | bytes 13341483 | solution.py:72
  237.9 6.1 %while.100 = (s32[]{:T(128)}, f32[2,58,1024]{1,2,0:T(8,128)S(1)}, s32[]{:T(128)}, f32[2,58,16]{1,2,0:T(8,128)S(1)}, s32[]{:T(128)}, /*index=5*/f32[]{:T(128)}) while((s32[]{:T(128)}, f32[2,58,1024]{1,2,0:T(8,128)S(1)}, s32[]{:T(128)}, f32[2,58,16]{1,2,0:T(8,128)S(1)}, s32[]{:T(128)}, /*index=5*/f32[]{:T(128)}) %tuple.444), condition=%wide.region_24.25_spmd.clone.clone, body=%wide.region_22.24_spmd.clone.clone.sunk | while | flops 2201393 | bytes 13341483 | solution.py:72
  246.9 10.9 %while.99 = (s32[]{:T(128)}, f32[2,58,1024]{1,2,0:T(8,128)S(1)}, s32[]{:T(128)}, f32[2,58,16]{1,2,0:T(8,128)S(1)}, s32[]{:T(128)}, /*index=5*/f32[]{:T(128)}) while((s32[]{:T(128)}, f32[2,58,1024]{1,2,0:T(8,128)S(1)}, s32[]{:T(128)}, f32[2,58,16]{1,2,0:T(8,128)S(1)}, s32[]{:T(128)}, /*index=5*/f32[]{:T(128)}) %tuple.443), condition=%wide.region_19.20_spmd.clone.clone, body=%wide.region_17.19_spmd.clone.clone.sunk | while | flops 2201393 | bytes 13341483 | solution.py:72
  259.9 56.4 %while.98 = (s32[]{:T(128)}, f32[2,58,1024]{1,2,0:T(8,128)S(1)}, s32[]{:T(128)}, f32[2,58,16]{1,2,0:T(8,128)S(1)}, s32[]{:T(128)}, /*index=5*/f32[]{:T(128)}) while((s32[]{:T(128)}, f32[2,58,1024]{1,2,0:T(8,128)S(1)}, s32[]{:T(128)}, f32[2,58,16]{1,2,0:T(8,128)S(1)}, s32[]{:T(128)}, /*index=5*/f32[]{:T(128)}) %tuple.442), condition=%wide.region_14.15_spmd.clone.clone, body=%wide.region_12.14_spmd.clone.clone.sunk | while | flops 2201393 | bytes 13341483 | solution.py:72
  318.6 5.6 %while.97 = (s32[]{:T(128)}, f32[2,58,1024]{1,2,0:T(8,128)S(1)}, s32[]{:T(128)}, f32[2,58,16]{1,2,0:T(8,128)S(1)}, s32[]{:T(128)}, /*index=5*/f32[]{:T(128)}) while((s32[]{:T(128)}, f32[2,58,1024]{1,2,0:T(8,128)S(1)}, s32[]{:T(128)}, f32[2,58,16]{1,2,0:T(8,128)S(1)}, s32[]{:T(128)}, /*index=5*/f32[]{:T(128)}) %tuple.441), condition=%wide.region_9.10_spmd.clone.clone, body=%wide.region_7.9_spmd.clone.clone.sunk | while | flops 2201393 | bytes 13341483 | solution.py:72
  326.5 10.7 %while.96 = (s32[]{:T(128)}, f32[2,58,1024]{1,2,0:T(8,128)S(1)}, s32[]{:T(128)}, f32[2,58,16]{1,2,0:T(8,128)S(1)}, s32[]{:T(128)}, /*index=5*/f32[]{:T(128)}) while((s32[]{:T(128)}, f32[2,58,1024]{1,2,0:T(8,128)S(1)}, s32[]{:T(128)}, f32[2,58,16]{1,2,0:T(8,128)S(1)}, s32[]{:T(128)}, /*index=5*/f32[]{:T(128)}) %tuple.440), condition=%wide.region_4.5_spmd.clone.clone, body=%wide.region_2.4_spmd.clone.clone.sunk | while | flops 2201393 | bytes 13341483 | solution.py:72
  340.7 19.4 %all-to-all-start.3 = ((f32[2,58,1,128]{1,0,2,3:T(2,128)}), f32[2,58,1,128]{1,0,2,3:T(2,128)S(1)}, u32[]{:S(2)}, u32[]{:S(2)}) async-start(f32[2,58,1,128]{1,0,2,3:T(2,128)} %bitcast.44), calls=%async_computation.3 | async-start | bytes 262144 | tf_op jit(solution)/shard_map/all_to_all | solution.py:150
  360.1 2.5 constant_dynamic-update-slice_fusion.15
  362.6 2.3 constant_dynamic-update-slice_fusion.14
  364.9 2.3 constant_dynamic-update-slice_fusion.13
  367.2 2.3 constant_dynamic-update-slice_fusion.12
  373.8 7.8 %gather_fusion.10 = f32[128,2,58,64]{3,2,1,0:T(8,128)} fusion(f32[2,58,64,128]{2,1,0,3:T(8,128)} %constant_dynamic-update-slice_fusion.8, s32[1024]{0:T(1024)} %copy-done.28), kind=kCustom, calls=%fused_computation.10 | custom fusion | bytes 7602688 | tf_op jit(solution)/shard_map/gather | solution.py:146
  381.7 13.9 %copy.781 = f32[2,58,64,128]{2,0,1,3:T(2,128)} copy(f32[2,58,64,128]{2,1,0,3:T(8,128)} %bitcast.211) | data formatting | bytes 7602176 | tf_op jit(solution)/shard_map/gather | solution.py:146
  395.5 10.2 %reshape.768 = f32[128,1,7424]{2,1,0:T(1,128)} reshape(f32[128,58,2,64]{3,2,1,0:T(2,128)} %bitcast.206) | data formatting | bytes 7602176
  405.7 10.5 %all-to-all-start.4 = ((f32[128,1,7424]{2,1,0:T(1,128)}), f32[128,1,7424]{2,1,0:T(1,128)}, u32[]{:S(2)}, u32[]{:S(2)}) async-start(f32[128,1,7424]{2,1,0:T(1,128)} %reshape.768), calls=%async_computation.4 | async-start | bytes 7602176 | tf_op jit(solution)/shard_map/all_to_all | solution.py:149
  417.7 46.8 %all-to-all-done.4 = f32[128,1,7424]{2,1,0:T(1,128)} async-done(((f32[128,1,7424]{2,1,0:T(1,128)}), f32[128,1,7424]{2,1,0:T(1,128)}, u32[]{:S(2)}, u32[]{:S(2)}) %all-to-all-start.4) | async-done | bytes 3801120 | tf_op jit(solution)/shard_map/all_to_all | solution.py:149
  464.5 13.1 %reduce.3 = f32[128,7424]{1,0:T(8,128)} reduce(f32[128,1,7424]{2,1,0:T(1,128)} %all-to-all-done.4, f32[]{:T(128)} %broadcast.1129), dimensions={1}, to_apply=%all_to_all.23.reduce_sub_computation | reduce | bytes 7602180 | tf_op jit(solution)/shard_map/all_to_all | solution.py:149
  477.6 8.6 %reshape.769 = f32[128,58,2,64]{3,2,1,0:T(2,128)} reshape(f32[128,7424]{1,0:T(8,128)} %reduce.3) | data formatting | bytes 7602176
  486.2 7.7 %copy.736 = f32[2,58,64,128]{2,1,0,3:T(8,128)} copy(f32[2,58,64,128]{2,0,1,3:T(2,128)} %bitcast.207) | data formatting | bytes 7602176 | tf_op jit(solution)/shard_map/all_to_all | solution.py:149
  493.9 7.8 %gather_fusion.11 = f32[128,2,58,64]{3,2,1,0:T(8,128)} fusion(f32[2,58,64,128]{2,1,0,3:T(8,128)} %copy.736, s32[1024]{0:T(1024)} %get-tuple-element.1063), kind=kCustom, calls=%fused_computation.11 | custom fusion | bytes 7602688 | tf_op jit(solution)/shard_map/gather | solution.py:152
  501.7 7.9 %copy.738 = f32[2,58,64,128]{3,2,1,0:T(8,128)} copy(f32[2,58,64,128]{2,1,0,3:T(8,128)} %bitcast.208) | data formatting | bytes 7602176
  (481 shorter events, 126.1 us)
Async XLA Ops:
  3.7 38.0 %collective-permute-start.1 = (f32[2,72,256]{1,0,2:T(2,128)S(1)}, f32[2,72,256]{1,0,2:T(2,128)S(1)}, u32[]{:S(2)}, u32[]{:S(2)}) collective-permute-start(f32[2,72,256]{1,0,2:T(2,128)S(1)} %bitcast.212), channel_id=1, source_target_pairs={{1,0},{2,1},{3,2},{4,3},{5,4},{6,5},{7,6},{8,7},{9,8},{10,9},{11,1... | collective-permute-start | bytes 442376 | tf_op jit(solution)/shard_map/ppermute | solution.py:21
  11.9 29.7 %collective-permute-start = (f32[2,72,256]{1,0,2:T(2,128)S(1)}, f32[2,72,256]{1,0,2:T(2,128)S(1)}, u32[]{:S(2)}, u32[]{:S(2)}) collective-permute-start(f32[2,72,256]{1,0,2:T(2,128)S(1)} %bitcast.213), channel_id=1, source_target_pairs={{0,1},{1,2},{2,3},{3,4},{4,5},{5,6},{6,7},{7,8},{8,9},{9,10},{10,1... | collective-permute-start | bytes 442376 | tf_op jit(solution)/shard_map/ppermute | solution.py:20
  15.2 11.5 %copy-start.28 = (s32[1024]{0:T(1024)}, s32[1024]{0:T(1024)S(1)}, u32[]{:S(2)}) copy-start(s32[1024]{0:T(1024)S(1)} %pad_clamp_fusion.3) | copy-start | bytes 12292
  17.5 18.3 %all-to-all-start = ((s32[128,1,1]{2,1,0:T(1,128)}), s32[128,1,1]{2,1,0:T(1,128)S(1)}, u32[]{:S(2)}, u32[]{:S(2)}) async-start(s32[128,1,1]{2,1,0:T(1,128)} %copy.693), calls=%async_computation | async-start | bytes 131072 | tf_op jit(solution)/shard_map/all_to_all | solution.py:134
  45.4 0.7 copy-start.9
  48.9 45.8 %all-to-all-start.2 = ((f32[2,58,1,128]{1,0,2,3:T(2,128)}), f32[2,58,1,128]{1,0,2,3:T(2,128)S(1)}, u32[]{:S(2)}, u32[]{:S(2)}) async-start(f32[2,58,1,128]{1,0,2,3:T(2,128)} %bitcast.17), calls=%async_computation.2 | async-start | bytes 262144 | tf_op jit(solution)/shard_map/all_to_all | solution.py:141
  84.5 23.1 %copy-start.27 = (s32[8]{0:T(128)S(1)}, s32[8]{0:T(128)}, u32[]{:S(2)}) copy-start(s32[8]{0:T(128)} %param.28) | copy-start | bytes 100
  94.7 58.6 %all-to-all-start.1 = ((f32[128,1,7424]{2,1,0:T(1,128)}), f32[128,1,7424]{2,1,0:T(1,128)}, u32[]{:S(2)}, u32[]{:S(2)}) async-start(f32[128,1,7424]{2,1,0:T(1,128)} %reshape.766), calls=%async_computation.1 | async-start | bytes 7602176 | tf_op jit(solution)/shard_map/all_to_all | solution.py:140
  224.7 13.2 %copy-start.14 = (f32[2,58,16]{1,2,0:T(8,128)S(1)}, f32[2,58,16]{1,2,0:T(8,128)}, u32[]{:S(2)}) copy-start(f32[2,58,16]{1,2,0:T(8,128)} %copy.713) | copy-start | bytes 22276
  237.9 8.3 %copy-start.4 = (f32[2,58,64,16]{2,1,0,3:T(8,128)S(1)}, f32[2,58,64,16]{2,1,0,3:T(8,128)}, u32[]{:S(2)}) copy-start(f32[2,58,64,16]{2,1,0,3:T(8,128)} %get-tuple-element.1039) | copy-start | bytes 1425412
  237.9 8.9 %copy-start.13 = (f32[2,58,16]{1,2,0:T(8,128)S(1)}, f32[2,58,16]{1,2,0:T(8,128)}, u32[]{:S(2)}) copy-start(f32[2,58,16]{1,2,0:T(8,128)} %copy.710) | copy-start | bytes 22276
  246.8 12.5 %copy-start.3 = (f32[2,58,64,16]{2,1,0,3:T(8,128)S(1)}, f32[2,58,64,16]{2,1,0,3:T(8,128)}, u32[]{:S(2)}) copy-start(f32[2,58,64,16]{2,1,0,3:T(8,128)} %get-tuple-element.1040) | copy-start | bytes 1425412
  246.8 13.1 %copy-start.12 = (f32[2,58,16]{1,2,0:T(8,128)S(1)}, f32[2,58,16]{1,2,0:T(8,128)}, u32[]{:S(2)}) copy-start(f32[2,58,16]{1,2,0:T(8,128)} %copy.707) | copy-start | bytes 22276
  259.9 58.1 %copy-start.2 = (f32[2,58,64,16]{2,1,0,3:T(8,128)S(1)}, f32[2,58,64,16]{2,1,0,3:T(8,128)}, u32[]{:S(2)}) copy-start(f32[2,58,64,16]{2,1,0,3:T(8,128)} %get-tuple-element.1041) | copy-start | bytes 1425412
  259.9 58.6 %copy-start.11 = (f32[2,58,16]{1,2,0:T(8,128)S(1)}, f32[2,58,16]{1,2,0:T(8,128)}, u32[]{:S(2)}) copy-start(f32[2,58,16]{1,2,0:T(8,128)} %copy.704) | copy-start | bytes 22276
  318.6 7.2 %copy-start.1 = (f32[2,58,64,16]{2,1,0,3:T(8,128)S(1)}, f32[2,58,64,16]{2,1,0,3:T(8,128)}, u32[]{:S(2)}) copy-start(f32[2,58,64,16]{2,1,0,3:T(8,128)} %get-tuple-element.1042) | copy-start | bytes 1425412
  318.6 7.8 %copy-start.10 = (f32[2,58,16]{1,2,0:T(8,128)S(1)}, f32[2,58,16]{1,2,0:T(8,128)}, u32[]{:S(2)}) copy-start(f32[2,58,16]{1,2,0:T(8,128)} %copy.701) | copy-start | bytes 22276
  326.4 12.5 %copy-start.26 = (f32[2,58,16]{1,0,2:T(2,128)S(1)}, f32[2,58,16]{1,0,2:T(2,128)}, u32[]{:S(2)}) copy-start(f32[2,58,16]{1,0,2:T(2,128)} %get-tuple-element.884) | copy-start | bytes 22276
  326.4 12.5 %copy-start.25 = (f32[2,58,16]{1,0,2:T(2,128)S(1)}, f32[2,58,16]{1,0,2:T(2,128)}, u32[]{:S(2)}) copy-start(f32[2,58,16]{1,0,2:T(2,128)} %get-tuple-element.885) | copy-start | bytes 22276
  326.4 12.5 %copy-start.24 = (f32[2,58,16]{1,0,2:T(2,128)S(1)}, f32[2,58,16]{1,0,2:T(2,128)}, u32[]{:S(2)}) copy-start(f32[2,58,16]{1,0,2:T(2,128)} %get-tuple-element.886) | copy-start | bytes 22276
  326.4 12.5 %copy-start.23 = (f32[2,58,16]{1,0,2:T(2,128)S(1)}, f32[2,58,16]{1,0,2:T(2,128)}, u32[]{:S(2)}) copy-start(f32[2,58,16]{1,0,2:T(2,128)} %get-tuple-element.887) | copy-start | bytes 22276
  326.5 12.5 %copy-start.18 = (f32[2,58,16]{1,2,0:T(8,128)S(1)}, f32[2,58,16]{1,2,0:T(8,128)}, u32[]{:S(2)}) copy-start(f32[2,58,16]{1,2,0:T(8,128)} %reduce_sum.224) | copy-start | bytes 22276
  326.5 12.5 %copy-start.22 = (f32[2,58,16]{1,0,2:T(2,128)S(1)}, f32[2,58,16]{1,0,2:T(2,128)}, u32[]{:S(2)}) copy-start(f32[2,58,16]{1,0,2:T(2,128)} %get-tuple-element.888) | copy-start | bytes 22276
  326.5 12.5 %copy-start.17 = (f32[2,58,16]{1,2,0:T(8,128)S(1)}, f32[2,58,16]{1,2,0:T(8,128)}, u32[]{:S(2)}) copy-start(f32[2,58,16]{1,2,0:T(8,128)} %reduce_sum.226) | copy-start | bytes 22276
  326.5 12.5 %copy-start.21 = (f32[2,58,16]{1,0,2:T(2,128)S(1)}, f32[2,58,16]{1,0,2:T(2,128)}, u32[]{:S(2)}) copy-start(f32[2,58,16]{1,0,2:T(2,128)} %get-tuple-element.889) | copy-start | bytes 22276
  326.5 12.5 %copy-start.16 = (f32[2,58,16]{1,2,0:T(8,128)S(1)}, f32[2,58,16]{1,2,0:T(8,128)}, u32[]{:S(2)}) copy-start(f32[2,58,16]{1,2,0:T(8,128)} %reduce_sum.228) | copy-start | bytes 22276
  326.5 12.5 %copy-start.20 = (f32[2,58,16]{1,0,2:T(2,128)S(1)}, f32[2,58,16]{1,0,2:T(2,128)}, u32[]{:S(2)}) copy-start(f32[2,58,16]{1,0,2:T(2,128)} %get-tuple-element.890) | copy-start | bytes 22276
  326.5 12.5 %copy-start.15 = (f32[2,58,16]{1,2,0:T(8,128)S(1)}, f32[2,58,16]{1,2,0:T(8,128)}, u32[]{:S(2)}) copy-start(f32[2,58,16]{1,2,0:T(8,128)} %reduce_sum.230) | copy-start | bytes 22276
  326.5 12.5 %copy-start.19 = (f32[2,58,16]{1,0,2:T(2,128)S(1)}, f32[2,58,16]{1,0,2:T(2,128)}, u32[]{:S(2)}) copy-start(f32[2,58,16]{1,0,2:T(2,128)} %get-tuple-element.883) | copy-start | bytes 22276
  337.2 33.4 %copy-start.7 = (f32[2,58,64,16]{2,1,0,3:T(8,128)S(1)}, f32[2,58,64,16]{2,1,0,3:T(8,128)}, u32[]{:S(2)}) copy-start(f32[2,58,64,16]{2,1,0,3:T(8,128)} %copy.732) | copy-start | bytes 1425412
  337.3 34.5 %copy-start.6 = (f32[2,58,64,16]{2,1,0,3:T(8,128)S(1)}, f32[2,58,64,16]{2,1,0,3:T(8,128)}, u32[]{:S(2)}) copy-start(f32[2,58,64,16]{2,1,0,3:T(8,128)} %copy.733) | copy-start | bytes 1425412
  338.9 33.9 %copy-start.5 = (f32[2,58,64,16]{2,1,0,3:T(8,128)S(1)}, f32[2,58,64,16]{2,1,0,3:T(8,128)}, u32[]{:S(2)}) copy-start(f32[2,58,64,16]{2,1,0,3:T(8,128)} %copy.734) | copy-start | bytes 1425412
  340.7 65.0 %all-to-all-start.3 = ((f32[2,58,1,128]{1,0,2,3:T(2,128)}), f32[2,58,1,128]{1,0,2,3:T(2,128)S(1)}, u32[]{:S(2)}, u32[]{:S(2)}) async-start(f32[2,58,1,128]{1,0,2,3:T(2,128)} %bitcast.44), calls=%async_computation.3 | async-start | bytes 262144 | tf_op jit(solution)/shard_map/all_to_all | solution.py:150
  360.1 9.4 %copy-start.8 = (f32[2,58,64,16]{2,1,0,3:T(8,128)S(1)}, f32[2,58,64,16]{2,1,0,3:T(8,128)}, u32[]{:S(2)}) copy-start(f32[2,58,64,16]{2,1,0,3:T(8,128)} %copy.731) | copy-start | bytes 1425412
  395.5 20.7 %copy-start = (s32[128]{0:T(128)S(1)}, s32[128]{0:T(128)}, u32[]{:S(2)}) copy-start(s32[128]{0:T(128)} %get-tuple-element.1052) | copy-start | bytes 1540
  405.7 58.8 %all-to-all-start.4 = ((f32[128,1,7424]{2,1,0:T(1,128)}), f32[128,1,7424]{2,1,0:T(1,128)}, u32[]{:S(2)}, u32[]{:S(2)}) async-start(f32[128,1,7424]{2,1,0:T(1,128)} %reshape.768), calls=%async_computation.4 | async-start | bytes 7602176 | tf_op jit(solution)/shard_map/all_to_all | solution.py:149
where the time goes:
time: 518 us; the launch traced here: 510 us
  local copies, waits for them, and re-layouts  230 us (44%)
  waiting for transfers between devices  89.8 us (17%)
  other arithmetic  89.2 us (17%)
  starting transfers between devices  62.6 us (12%)
  loops' own time  35.4 us (7%)
    unnamed x81, local copies, waits for them, and re-layouts  72.9 us
    all_to_all x1, waiting for transfers between devices, on_device(): lax.all_to_all(back_state, 'dev', split_axis=3, concat_axis=3, tiled=True)  46.8 us
    all_to_all x1, waiting for transfers between devices, on_device(): lax.all_to_all(send_state, 'dev', split_axis=3, concat_axis=3, tiled=True)  37.6 us
    another operation x8, loops' own time, cloud_step(): lax.fori_loop(0, trip_count, substep, flat)  35.4 us
    gather x2, local copies, waits for them, and re-layouts, on_device(): back_state = new_slots[..., sorted_slots]  21.7 us
    gather x2, local copies, waits for them, and re-layouts, on_device(): send_state = cloud_state[..., asked_flat]  21.6 us
    all_to_all x1, starting transfers between devices, on_device(): lax.all_to_all(back_tend, 'dev', split_axis=3, concat_axis=3, tiled=True)  19.4 us
    add x22, other arithmetic, substep(): diffused = relaxed + diffusion * laplace  19.3 us
  transfers between devices with their start and end apart: 7, of which 3 were waited for; matrix products, arithmetic and copies ran while one was open for 22% of the time, Pallas kernels for 0%

commit v1 on v0

v1 whole, which is shorter than its diff:
```python
import functools

import jax
import jax.numpy as jnp
from jax import lax
from jax.experimental import pallas as pl
from jax.experimental.pallas import tpu as pltpu
from jax.sharding import PartitionSpec as P

LANES = 128
ROWS = 8
GROUP = 8
PAD = 8
CHUNKS = 6
UNROLL = 58


def odious(node):
    return ((node ^ (node >> 1) ^ (node >> 2) ^ (node >> 3)) & 1) == 1


def edge_of(node):
    return jnp.where(
        (node == 1) | (node == 2), 0, jnp.where((node == 7) | (node == 11), 1, jnp.where((node == 14) | (node == 13), 2, 3))
    )


def which_of(node):
    return jnp.where((node == 2) | (node == 11) | (node == 13) | (node == 4), 1, 0)


def lanes(shape=(ROWS, LANES)):
    return lax.broadcasted_iota(jnp.int32, shape, len(shape) - 1)


def total_of(parts):
    while len(parts) > 1:
        parts = [a + b for a, b in zip(parts[::2], parts[1::2])] + ([parts[-1]] if len(parts) % 2 else [])
    return parts[0]


def exchange_kernel(
    devices, span, dyn_ref, source_ref, sub_ref, halo_ref, count_ref, edges, outgoing, arrived, second, arrived2,
    halo_send, halo_recv, own_sem, one_send, one_recv, two_send, two_recv,
):
    me = lax.axis_index("dev")
    groups = devices // GROUP
    group = me // GROUP
    member = me % GROUP
    above = (me + 1) % devices
    below = (me + devices - 1) % devices

    barrier = pltpu.get_barrier_semaphore()
    for step in range(1, groups):
        pl.semaphore_signal(barrier, inc=1, device_id=(((group + step) % groups) * GROUP + member,), device_id_type=pl.DeviceIdType.MESH)
    for step in range(1, GROUP):
        pl.semaphore_signal(barrier, inc=1, device_id=(group * GROUP + (member + step) % GROUP,), device_id_type=pl.DeviceIdType.MESH)
    pl.semaphore_signal(barrier, inc=1, device_id=(above,), device_id_type=pl.DeviceIdType.MESH)
    pl.semaphore_signal(barrier, inc=1, device_id=(below,), device_id_type=pl.DeviceIdType.MESH)

    fields, levels, _ = dyn_ref.shape
    on_edge = odious(lanes((levels, LANES)) % 16)
    for f in range(fields):
        for j in range(2):
            first = dyn_ref[f, :, 2 * j * LANES : (2 * j + 1) * LANES]
            later = dyn_ref[f, :, (2 * j + 1) * LANES : (2 * j + 2) * LANES]
            edges[f, :, j * LANES : (j + 1) * LANES] = jnp.where(on_edge, first, pltpu.roll(later, 8, axis=1))

    spans = sub_ref.shape[0]
    slot = lanes((1, LANES))
    counts = jnp.zeros((1, LANES), jnp.int32)
    for i in range(spans):
        counts = jnp.where(slot // span == i, sub_ref[i], counts)
    source = source_ref[...]
    target = lax.broadcasted_iota(jnp.int32, (devices, LANES), 0)
    to_device = jnp.where(source // LANES == target, counts, 0).astype(jnp.float32).astype(jnp.bfloat16)
    row = lax.broadcasted_iota(jnp.int32, (LANES, LANES), 0)
    to_lane = jnp.where(source % LANES == row, 1.0, 0.0).astype(jnp.bfloat16)
    message = lax.dot_general(to_device, to_lane, (((1,), (1,)), ((), ())), preferred_element_type=jnp.float32)
    outgoing[...] = message.astype(jnp.int32).reshape(groups, GROUP, LANES)

    pl.semaphore_wait(barrier, groups - 1 + GROUP - 1 + 2)

    copies = []

    def send(src, dst, send_sem, recv_sem, device):
        copy = pltpu.make_async_remote_copy(
            src_ref=src, dst_ref=dst, send_sem=send_sem, recv_sem=recv_sem, device_id=(device,), device_id_type=pl.DeviceIdType.MESH
        )
        copy.start()
        return copy

    copies.append(send(edges, halo_ref.at[1], halo_send.at[0], halo_recv.at[0], above))
    copies.append(send(edges, halo_ref.at[2], halo_send.at[1], halo_recv.at[1], below))
    own = pltpu.make_async_copy(edges, halo_ref.at[0], own_sem)
    own.start()
    firsts = []
    for step in range(1, groups):
        to = (group + step) % groups
        firsts.append(send(outgoing.at[to], arrived.at[step], one_send.at[step], one_recv.at[step], to * GROUP + member))
    for copy in firsts:
        copy.wait_recv()
    merged = outgoing[group]
    for step in range(1, groups):
        merged = merged + arrived[step]
    for q in range(GROUP):
        second[q] = jnp.broadcast_to(merged[q : q + 1, :], (ROWS, LANES))
    seconds = []
    for step in range(1, GROUP):
        to = (member + step) % GROUP
        seconds.append(send(second.at[to], arrived2.at[step], two_send.at[step], two_recv.at[step], group * GROUP + to))
    for copy in seconds:
        copy.wait_recv()
    mine = second[member]
    for step in range(1, GROUP):
        mine = mine + arrived2[step]
    count_ref[...] = mine
    for copy in firsts + seconds:
        copy.wait_send()
    for copy in copies:
        copy.wait()
    own.wait()


def exchange(dynamics, span_source, substeps, devices):
    fields, levels, nodes = dynamics.shape
    groups = devices // GROUP
    span = span_source.shape[0] // substeps.shape[0]
    return pl.pallas_call(
        functools.partial(exchange_kernel, devices, span),
        out_shape=(
            jax.ShapeDtypeStruct((3, fields, levels, nodes // 2), jnp.float32),
            jax.ShapeDtypeStruct((ROWS, LANES), jnp.int32),
        ),
        in_specs=[
            pl.BlockSpec(memory_space=pltpu.VMEM),
            pl.BlockSpec(memory_space=pltpu.VMEM),
            pl.BlockSpec(memory_space=pltpu.SMEM),
        ],
        out_specs=(pl.BlockSpec(memory_space=pl.ANY), pl.BlockSpec(memory_space=pltpu.VMEM)),
        scratch_shapes=[
            pltpu.VMEM((fields, levels, nodes // 2), jnp.float32),
            pltpu.VMEM((groups, GROUP, LANES), jnp.int32),
            pltpu.VMEM((groups, GROUP, LANES), jnp.int32),
            pltpu.VMEM((GROUP, ROWS, LANES), jnp.int32),
            pltpu.VMEM((GROUP, ROWS, LANES), jnp.int32),
            pltpu.SemaphoreType.DMA((2,)),
            pltpu.SemaphoreType.DMA((2,)),
            pltpu.SemaphoreType.DMA,
            pltpu.SemaphoreType.DMA((groups,)),
            pltpu.SemaphoreType.DMA((groups,)),
            pltpu.SemaphoreType.DMA((GROUP,)),
            pltpu.SemaphoreType.DMA((GROUP,)),
        ],
        compiler_params=pltpu.CompilerParams(collective_id=0, has_side_effects=True, vmem_limit_bytes=8 * 2**20),
        name="exchange",
    )(dynamics, span_source.reshape(1, -1), substeps)


def split_dot(values, weights):
    upper = values.astype(jnp.bfloat16)
    lower = (values - upper.astype(jnp.float32)).astype(jnp.bfloat16)
    return jnp.dot(upper, weights, preferred_element_type=jnp.float32) + jnp.dot(lower, weights, preferred_element_type=jnp.float32)


def edge_sum(me, devices, dyn_ref, halo, adj_ref, dsum_ref, force_ref):
    fields, levels, nodes = dyn_ref.shape
    rows = fields * levels
    half = nodes // 2
    elements = nodes // 16
    across = jnp.broadcast_to(adj_ref[0:1, :], (ROWS, LANES))
    facing = jnp.broadcast_to(adj_ref[1:2, :], (ROWS, LANES))
    block = (across // elements - me + devices) % devices
    part = jnp.where(block == 0, 0, jnp.where(block == 1, 2, 1))
    positions = []
    for t in range(2):
        other = ((2, 1), (11, 7), (13, 14), (4, 8))
        node = jnp.where(
            facing == 0, other[0][t], jnp.where(facing == 1, other[1][t], jnp.where(facing == 2, other[2][t], other[3][t]))
        )
        place = (across % elements) * 16 + node
        in_pair = place % 256
        lane = jnp.where(in_pair < LANES, in_pair, (in_pair - LANES + 8) % LANES)
        positions.append(part * half + (place // 256) * LANES + lane)

    lane = lanes()
    node = lane % 16
    on_edge = odious(node)
    landing = []
    for v in range(nodes // LANES):
        index = 32 * v + 4 * (lane // 16) + edge_of(node)
        picked = [jnp.take_along_axis(p, index, axis=1, mode="promise_in_bounds") for p in positions]
        landing.append(jnp.where(on_edge, jnp.where(which_of(node) == 0, picked[0], picked[1]), -1)[0:1])
    landing = jnp.concatenate(landing, axis=1)
    row = lax.broadcasted_iota(jnp.int32, (3 * half, nodes), 0)
    weights = jnp.where(row == landing, 1.0, 0.0).astype(jnp.bfloat16)

    edge_values = jnp.concatenate([halo[i].reshape(rows, half) for i in range(3)], axis=1)
    own = dyn_ref[...].reshape(rows, nodes)

    quarter = lane % 4
    base = lane - quarter

    def pick(t, edge):
        return jnp.take_along_axis(positions[t], base + edge, axis=1, mode="promise_in_bounds")

    def by_quarter(options):
        a, b, c, d = options
        return jnp.where(quarter == 0, a, jnp.where(quarter == 1, b, jnp.where(quarter == 2, c, d)))[0:1]

    one = by_quarter([pick(0, 0), pick(1, 0), pick(0, 3), pick(1, 1)])
    two = by_quarter([pick(1, 3), pick(0, 1), pick(1, 2), pick(0, 2)])
    row = lax.broadcasted_iota(jnp.int32, (3 * half, LANES), 0)
    across_weights = jnp.where((row == one) | (row == two), 0.125, 0.0).astype(jnp.bfloat16)
    row = lax.broadcasted_iota(jnp.int32, (nodes, LANES), 0)
    inner = row % 16
    column = 4 * (row // 16) + 2 * (inner // 8) + (inner % 4) // 2
    own_weights = jnp.where(
        column == lax.broadcasted_iota(jnp.int32, (nodes, LANES), 1), jnp.where(odious(inner), 0.125, 0.25), 0.0
    ).astype(jnp.bfloat16)
    force_ref[...] = split_dot(own, own_weights) + split_dot(edge_values, across_weights)

    opposite = split_dot(edge_values, weights)
    edge_lane = odious(lanes((rows, nodes)) % 16)
    dsum_ref[...] = jnp.where(edge_lane, 0.5 * (own + opposite), own).reshape(fields, levels, nodes)


def columns_kernel(
    devices, bounds, dyn_ref, halo_ref, adj_ref, count_ref, cloud_ref, dsum_ref, tend_ref, new_ref,
    state, halo, force, sums, mean_e, mean_a, term_e, term_a, bias, bias_a, old_e, old_a, in_sems, out_sems, halo_sem,
):
    depth = cloud_ref.shape[1]
    levels = dyn_ref.shape[1]
    width = cloud_ref.shape[2]
    parts = width // ROWS
    top = mean_e.shape[0] - 2 * PAD
    me = lax.axis_index("dev")

    loads = []
    halo_copy = pltpu.make_async_copy(halo_ref, halo, halo_sem)
    halo_copy.start()
    for i, (lo, hi) in enumerate(bounds):
        copy = pltpu.make_async_copy(cloud_ref.at[:, lo:hi], state.at[:, lo:hi], in_sems.at[i])
        copy.start()
        loads.append(copy)
    halo_copy.wait()
    edge_sum(me, devices, dyn_ref, halo, adj_ref, dsum_ref, force)

    height = lax.broadcasted_iota(jnp.int32, (top, LANES), 0).astype(jnp.float32)
    saturation = 0.8 * jnp.exp(-2.0 * height / depth)
    force_0 = force[0:top]
    force_1 = force[levels : levels + top]
    force_e = force_1 - 0.5 * force_0
    force_a = force_0 + force_1

    def begin(z, carry):
        total_a, total_e = [], []
        for k in range(parts):
            u0 = state[0, z, pl.ds(k, ROWS, stride=parts), :]
            u1 = state[1, z, pl.ds(k, ROWS, stride=parts), :]
            total_a.append(u0 + u1)
            total_e.append(u1 - 0.5 * u0)
        for k in range(parts):
            state[0, z, k * ROWS : (k + 1) * ROWS, :] = total_a[k]
            state[1, z, k * ROWS : (k + 1) * ROWS, :] = total_e[k]
        at = pl.multiple_of(z * ROWS, ROWS)
        sums[0, pl.ds(at, ROWS), :] = total_of(total_a)
        sums[1, pl.ds(at, ROWS), :] = total_of(total_e)
        return carry

    for (lo, hi), copy in zip(bounds, loads):
        copy.wait()
        lax.fori_loop(lo, hi, begin, 0, unroll=2)

    def mean_of(which):
        blocks = []
        for block in range(top // ROWS):
            start = block * ROWS * ROWS
            blocks.append(total_of([sums[which, pl.ds(start + j, ROWS, stride=ROWS), :] for j in range(ROWS)]))
        return jnp.concatenate(blocks, axis=0) * (1.0 / width)

    def spread(ref, values):
        ref[PAD : PAD + top, :] = values
        ref[PAD - 1 : PAD, :] = values[0:1]
        ref[PAD + depth : PAD + depth + 1, :] = values[depth - 1 : depth]
        return 8.0 * values + ref[PAD - 1 : PAD - 1 + top, :] + ref[PAD + 1 : PAD + 1 + top, :]

    def sweep(which, active, with_bias, with_sum, limit, unroll):
        def load(z):
            return [state[which, z, k * ROWS : (k + 1) * ROWS, :] for k in range(parts)]

        def level(z, before, here):
            after = load(jnp.minimum(z + 1, depth - 1) if not isinstance(z, int) else min(z + 1, depth - 1))
            left = pltpu.roll(here[parts - 1], 1, axis=0)
            right = pltpu.roll(here[0], ROWS - 1, axis=0)
            if with_bias is not None:
                shift = jnp.broadcast_to(with_bias[pl.ds(z, 1), :], (ROWS, LANES))
            stepped = []
            for k in range(parts):
                beside = (here[k - 1] if k > 0 else left) + (here[k + 1] if k < parts - 1 else right)
                value = 6.0 * here[k] + (beside + (before[k] + after[k]))
                if with_bias is not None:
                    value = value + shift
                if limit:
                    value = jnp.minimum(value, 0.25 * value)
                if active is not None:
                    value = jnp.where(active, value, here[k])
                stepped.append(value)
                state[which, z, k * ROWS : (k + 1) * ROWS, :] = value
            if with_sum:
                at = z * ROWS if isinstance(z, int) else pl.multiple_of(z * ROWS, ROWS)
                sums[which, pl.ds(at, ROWS), :] = total_of(stepped)
            return here, after

        before = here = load(0)
        if unroll >= depth:
            for z in range(depth):
                before, here = level(z, before, here)
            return
        whole = depth // unroll

        def several(i, carry):
            before, here = carry
            for j in range(unroll):
                before, here = level(i * unroll + j, before, here)
            return before, here

        before, here = lax.fori_loop(0, whole, several, (before, here))
        for z in range(whole * unroll, depth):
            before, here = level(z, before, here)

    counts = count_ref[...]
    least = jnp.min(counts)
    most = jnp.max(counts)

    start_a = mean_of(0)
    start_e = mean_of(1)
    old_a[...] = start_a
    old_e[...] = start_e
    term_e[...] = spread(mean_e, saturation + 0.3 * (force_e - saturation)) - 10.0 * saturation
    bias[...] = spread(mean_e, 0.3 * (force_e - start_e)) - 10.0 * saturation
    bias_a[...] = -spread(mean_a, start_a)
    term_a[...] = 0.3 * force_a
    mean_a_now = 0.1 * spread(mean_a, 0.7 * start_a + 0.3 * force_a)
    mean_a[PAD : PAD + top, :] = mean_a_now
    sweep(0, None, bias_a, False, False, UNROLL)
    sweep(1, None, bias, True, True, UNROLL)

    def profiles(scale, active):
        bias[...] = scale * term_e[...] - 0.3 * spread(mean_e, mean_of(1))
        now = mean_a[PAD : PAD + top, :]
        later = 0.1 * spread(mean_a, 0.7 * now + term_a[...])
        if active is not None:
            later = jnp.where(active, later, now)
        mean_a[PAD : PAD + top, :] = later

    def plain(step, scale):
        profiles(scale, None)
        sweep(0, None, None, False, False, UNROLL)
        sweep(1, None, bias, True, True, UNROLL)
        return scale * 10.0

    def masked(step, scale):
        active = counts > step
        profiles(scale, jnp.broadcast_to(active[0:1], (top, LANES)))
        sweep(0, active, None, False, False, UNROLL)
        sweep(1, active, bias, True, True, UNROLL)
        return scale * 10.0

    scale = lax.fori_loop(1, least, plain, jnp.float32(10.0))
    lax.fori_loop(least, most, masked, scale)

    shrink = jnp.ones((ROWS, LANES), jnp.float32)
    for step in range(12):
        shrink = jnp.where(counts > step, shrink * 0.1, shrink)
    across = shrink[0:1]
    new_a = mean_a[PAD : PAD + top, :]
    new_e = mean_of(1) * across + saturation
    tend_0 = (2.0 / 3.0) * ((new_a - new_e) - (old_a[...] - old_e[...]))
    tend_1 = (new_a - old_a[...]) - tend_0
    tend_ref[0] = tend_0[0:depth]
    tend_ref[1] = tend_1[0:depth]
    bias[...] = (2.0 / 3.0) * (new_a - saturation)
    bias_a[...] = new_a
    shrink_0 = (2.0 / 3.0) * shrink

    def finish(z, carry):
        add_0 = jnp.broadcast_to(bias[pl.ds(z, 1), :], (ROWS, LANES))
        add_a = jnp.broadcast_to(bias_a[pl.ds(z, 1), :], (ROWS, LANES))
        new_0, new_1 = [], []
        for k in range(parts):
            a = state[0, z, k * ROWS : (k + 1) * ROWS, :]
            e = state[1, z, k * ROWS : (k + 1) * ROWS, :]
            u0 = (a - e) * shrink_0 + add_0
            new_0.append(u0)
            new_1.append((a * shrink + add_a) - u0)
        for k in range(parts):
            state[0, z, pl.ds(k, ROWS, stride=parts), :] = new_0[k]
            state[1, z, pl.ds(k, ROWS, stride=parts), :] = new_1[k]
        return carry

    stores = []
    for i, (lo, hi) in enumerate(bounds):
        lax.fori_loop(lo, hi, finish, 0, unroll=2)
        copy = pltpu.make_async_copy(state.at[:, lo:hi], new_ref.at[:, lo:hi], out_sems.at[i])
        copy.start()
        stores.append(copy)
    for copy in stores:
        copy.wait()


def columns(dynamics, halo, adjacency, counts, cloud_state, devices):
    fields, levels, nodes = dynamics.shape
    depth, width = cloud_state.shape[1], cloud_state.shape[2]
    top = -(-depth // ROWS) * ROWS
    cuts = [round(i * depth / CHUNKS) for i in range(CHUNKS + 1)]
    bounds = tuple(zip(cuts[:-1], cuts[1:]))
    vmem = pl.BlockSpec(memory_space=pltpu.VMEM)
    anywhere = pl.BlockSpec(memory_space=pl.ANY)
    profile = pltpu.VMEM((top, LANES), jnp.float32)
    padded = pltpu.VMEM((top + 2 * PAD, LANES), jnp.float32)
    return pl.pallas_call(
        functools.partial(columns_kernel, devices, bounds),
        out_shape=(
            jax.ShapeDtypeStruct(dynamics.shape, jnp.float32),
            jax.ShapeDtypeStruct((fields, depth, LANES), jnp.float32),
            jax.ShapeDtypeStruct(cloud_state.shape, jnp.float32),
        ),
        in_specs=[vmem, anywhere, vmem, vmem, anywhere],
        out_specs=(vmem, vmem, anywhere),
        scratch_shapes=[
            pltpu.VMEM(cloud_state.shape, jnp.float32),
            pltpu.VMEM(halo.shape, jnp.float32),
            pltpu.VMEM((fields * levels, LANES), jnp.float32),
            pltpu.VMEM((2, top * ROWS, LANES), jnp.float32),
            padded, padded, profile, profile, profile, profile, profile, profile,
            pltpu.SemaphoreType.DMA((CHUNKS,)),
            pltpu.SemaphoreType.DMA((CHUNKS,)),
            pltpu.SemaphoreType.DMA,
        ],
        compiler_params=pltpu.CompilerParams(vmem_limit_bytes=40 * 2**20),
        name="columns",
    )(dynamics, halo, adjacency, counts, cloud_state)


def on_device(dynamics, adjacency, cloud_state, span_source, substeps):
    devices = lax.axis_size("dev")
    halo, counts = exchange(dynamics, span_source, substeps, devices)
    return columns(dynamics, halo, adjacency, counts, cloud_state, devices)


def solution(mesh):
    in_specs = (
        P(None, None, "dev"),
        P(None, "dev"),
        P(None, None, None, "dev"),
        P("dev"),
        P("dev"),
    )
    out_specs = (P(None, None, "dev"), P(None, None, "dev"), P(None, None, None, "dev"))
    return jax.shard_map(on_device, mesh=mesh, in_specs=in_specs, out_specs=out_specs, check_vma=False)
```

time: 518 us -> 40.8 us (0.08)
  the two profiles are of different devices: /device:TPU:0 before, /device:TPU:25 now
where the time goes in v1:
time: 40.8 us; the launch traced here: 40.5 us
  Pallas kernels  33.2 us (81%)
  local copies, waits for them, and re-layouts  6.65 us (16%)
  between operations  0.67 us (2%)
    pallas_call x1, Pallas kernels, columns(): pl.pallas_call(functools.partial(columns_kernel, devices, bounds), out_sh...  17.4 us
    pallas_call x1, Pallas kernels, exchange(): pl.pallas_call(functools.partial(exchange_kernel, devices, span), out_sha...  15.9 us
    unnamed x12, local copies, waits for them, and re-layouts  5.98 us

profile of v1, /device:TPU:25, one launch (start us, length us, event | category | flops | bytes accessed | tf_op | source)
XLA Modules:
  0.0 40.5 jit_solution(12482524206928293722)
XLA Ops:
  0.6 0.0 copy-start.1
  0.6 1.0 %copy-done.1 = f32[2,72,512]{2,1,0:T(8,128)S(1)} copy-done((f32[2,72,512]{2,1,0:T(8,128)S(1)}, f32[2,72,512]{2,1,0:T(8,128)}, u32[]{:S(2)}) %copy-start.1) | copy-done | bytes 294936
  1.6 0.0 copy-start.4
  1.6 0.7 %copy-done.4 = s32[128]{0:T(128)S(1)} copy-done((s32[128]{0:T(128)S(1)}, s32[128]{0:T(128)}, u32[]{:S(2)}) %copy-start.4) | copy-done | bytes 536
  2.3 0.0 copy-start.5
  2.3 0.7 %copy-done.5 = s32[8]{0:T(128)S(1)} copy-done((s32[8]{0:T(128)S(1)}, s32[8]{0:T(128)}, u32[]{:S(2)}) %copy-start.5) | copy-done | bytes 56
  2.9 15.9 %exchange.1 = (f32[3,2,72,256]{3,2,1,0:T(8,128)S(1)}, s32[8,128]{1,0:T(8,128)S(1)}) custom-call(f32[2,72,512]{2,1,0:T(8,128)S(1)} %copy-done.1, s32[1,128]{1,0:T(1,128)S(1)} %bitcast.1, s32[8]{0:T(128)S(1)} %copy-done.5), custom_call_target="tpu_custom_call" | custom-call | tf_op jit(solution)/shard_map/exchange/pallas_call | solution.py:129
  18.8 0.0 copy-start
  18.8 2.1 %copy-done = f32[2,58,64,128]{3,2,1,0:T(8,128)S(1)} copy-done((f32[2,58,64,128]{3,2,1,0:T(8,128)S(1)}, f32[2,58,64,128]{3,2,1,0:T(8,128)}, u32[]{:S(2)}) %copy-start) | copy-done | bytes 3801112
  20.8 0.0 copy-start.2
  20.9 1.0 %copy-done.2 = f32[2,72,512]{2,1,0:T(8,128)S(1)} copy-done((f32[2,72,512]{2,1,0:T(8,128)S(1)}, f32[2,72,512]{2,1,0:T(8,128)}, u32[]{:S(2)}) %copy-start.2) | copy-done | bytes 294936
  21.8 0.0 copy-start.3
  21.8 0.7 %copy-done.3 = s32[2,128]{1,0:T(2,128)S(1)} copy-done((s32[2,128]{1,0:T(2,128)S(1)}, s32[2,128]{1,0:T(2,128)}, u32[]{:S(2)}) %copy-start.3) | copy-done | bytes 1048
  22.5 17.4 %columns.1 = (f32[2,72,512]{2,1,0:T(8,128)}, f32[2,58,128]{2,1,0:T(8,128)S(1)}, f32[2,58,64,128]{3,2,1,0:T(8,128)}) custom-call(f32[2,72,512]{2,1,0:T(8,128)S(1)} %copy-done.2, f32[3,2,72,256]{3,2,1,0:T(8,128)S(1)} %get-tuple-element.5.halo_ref, s32[2,128]{1,0:T(2,128)S(1)} %copy-done.3, s32[8,128]{1,0:T(8,128)S(1)} %get-tuple-element.6.count_ref, ...), custom_call_target="tpu_custom_call" | custom-call | tf_op jit(solution)/shard_map/columns/pallas_call | solution.py:422
  39.9 0.7 %copy.8 = f32[2,58,128]{2,0,1:T(2,128)} copy(f32[2,58,128]{2,1,0:T(8,128)S(1)} %get-tuple-element.8) | data formatting | bytes 118784 | tf_op jit(solution)/shard_map/columns/pallas_call | solution.py:422
Async XLA Ops:
  0.6 1.0 %copy-start.1 = (f32[2,72,512]{2,1,0:T(8,128)S(1)}, f32[2,72,512]{2,1,0:T(8,128)}, u32[]{:S(2)}) copy-start(f32[2,72,512]{2,1,0:T(8,128)} %dyn_ref.3) | copy-start | bytes 884740
  1.6 0.7 %copy-start.4 = (s32[128]{0:T(128)S(1)}, s32[128]{0:T(128)}, u32[]{:S(2)}) copy-start(s32[128]{0:T(128)} %param.8) | copy-start | bytes 1540
  2.3 0.7 %copy-start.5 = (s32[8]{0:T(128)S(1)}, s32[8]{0:T(128)}, u32[]{:S(2)}) copy-start(s32[8]{0:T(128)} %sub_ref.1) | copy-start | bytes 100
  18.8 2.1 %copy-start = (f32[2,58,64,128]{3,2,1,0:T(8,128)S(1)}, f32[2,58,64,128]{3,2,1,0:T(8,128)}, u32[]{:S(2)}) copy-start(f32[2,58,64,128]{3,2,1,0:T(8,128)} %cloud_ref.1) | copy-start | bytes 11403268
  20.8 1.0 %copy-start.2 = (f32[2,72,512]{2,1,0:T(8,128)S(1)}, f32[2,72,512]{2,1,0:T(8,128)}, u32[]{:S(2)}) copy-start(f32[2,72,512]{2,1,0:T(8,128)} %dyn_ref.3) | copy-start | bytes 884740
  21.8 0.7 %copy-start.3 = (s32[2,128]{1,0:T(2,128)S(1)}, s32[2,128]{1,0:T(2,128)}, u32[]{:S(2)}) copy-start(s32[2,128]{1,0:T(2,128)} %adj_ref.1) | copy-start | bytes 3076

commit v2 on v1

v2 whole, which is shorter than its diff:
```python
import functools

import jax
import jax.numpy as jnp
from jax import lax
from jax.experimental import pallas as pl
from jax.experimental.pallas import tpu as pltpu
from jax.sharding import PartitionSpec as P

LANES = 128
ROWS = 8
GROUP = 8
PAD = 8
CHUNKS = 6
UNROLL = 58
SHORT = 2


def odious(node):
    return ((node ^ (node >> 1) ^ (node >> 2) ^ (node >> 3)) & 1) == 1


def edge_of(node):
    return jnp.where(
        (node == 1) | (node == 2), 0, jnp.where((node == 7) | (node == 11), 1, jnp.where((node == 14) | (node == 13), 2, 3))
    )


def which_of(node):
    return jnp.where((node == 2) | (node == 11) | (node == 13) | (node == 4), 1, 0)


def lanes(shape=(ROWS, LANES)):
    return lax.broadcasted_iota(jnp.int32, shape, len(shape) - 1)


def total_of(parts):
    while len(parts) > 1:
        parts = [a + b for a, b in zip(parts[::2], parts[1::2])] + ([parts[-1]] if len(parts) % 2 else [])
    return parts[0]


def mean_of(sums, width):
    blocks = []
    for start in range(0, sums.shape[0], ROWS * ROWS):
        blocks.append(total_of([sums[pl.ds(start + j, ROWS, stride=ROWS), :] for j in range(ROWS)]))
    return jnp.concatenate(blocks, axis=0) * (1.0 / width)


def spread(ref, values, depth):
    top = values.shape[0]
    ref[PAD : PAD + top, :] = values
    ref[PAD - 1 : PAD, :] = values[0:1]
    ref[PAD + depth : PAD + depth + 1, :] = values[depth - 1 : depth]
    return 8.0 * values + ref[PAD - 1 : PAD - 1 + top, :] + ref[PAD + 1 : PAD + 1 + top, :]


def saturation_of(top, depth):
    height = lax.broadcasted_iota(jnp.int32, (top, LANES), 0).astype(jnp.float32)
    return 0.8 * jnp.exp(-2.0 * height / depth)


def sweep(src, dst, which, active, bias, sums, limit, unroll):
    depth = src.shape[1]
    parts = src.shape[2] // ROWS

    def load(z):
        return [src[which, z, k * ROWS : (k + 1) * ROWS, :] for k in range(parts)]

    def level(z, before, here):
        known = isinstance(z, int)
        after = load(min(z + 1, depth - 1) if known else jnp.minimum(z + 1, depth - 1))
        left = pltpu.roll(here[parts - 1], 1, axis=0)
        right = pltpu.roll(here[0], ROWS - 1, axis=0)
        if bias is not None:
            shift = jnp.broadcast_to(bias[pl.ds(z, 1), :], (ROWS, LANES))
        stepped = []
        for k in range(parts):
            beside = (here[k - 1] if k > 0 else left) + (here[k + 1] if k < parts - 1 else right)
            value = 6.0 * here[k] + (beside + (before[k] + after[k]))
            if bias is not None:
                value = value + shift
            if limit:
                value = jnp.minimum(value, 0.25 * value)
            if active is not None:
                value = jnp.where(active, value, here[k])
            stepped.append(value)
            dst[which, z, k * ROWS : (k + 1) * ROWS, :] = value
        if sums is not None:
            at = z * ROWS if known else pl.multiple_of(z * ROWS, ROWS)
            sums[pl.ds(at, ROWS), :] = total_of(stepped)
        return here, after

    before = here = load(0)
    if unroll >= depth:
        for z in range(depth):
            before, here = level(z, before, here)
        return
    whole = depth // unroll

    def several(i, carry):
        before, here = carry
        for j in range(unroll):
            before, here = level(i * unroll + j, before, here)
        return before, here

    before, here = lax.fori_loop(0, whole, several, (before, here))
    for z in range(whole * unroll, depth):
        before, here = level(z, before, here)


def split_dot(values, weights):
    upper = values.astype(jnp.bfloat16)
    lower = (values - upper.astype(jnp.float32)).astype(jnp.bfloat16)
    return jnp.dot(upper, weights, preferred_element_type=jnp.float32) + jnp.dot(lower, weights, preferred_element_type=jnp.float32)


def partner_places(me, devices, adjacency, elements, half):
    across = jnp.broadcast_to(adjacency[0:1, :], (ROWS, LANES))
    facing = jnp.broadcast_to(adjacency[1:2, :], (ROWS, LANES))
    block = (across // elements - me + devices) % devices
    part = jnp.where(block == 0, 0, jnp.where(block == 1, 2, 1))
    places = []
    for t in range(2):
        other = ((2, 1), (11, 7), (13, 14), (4, 8))
        node = jnp.where(
            facing == 0, other[0][t], jnp.where(facing == 1, other[1][t], jnp.where(facing == 2, other[2][t], other[3][t]))
        )
        place = (across % elements) * 16 + node
        in_pair = place % 256
        lane = jnp.where(in_pair < LANES, in_pair, (in_pair - LANES + 8) % LANES)
        places.append(part * half + (place // 256) * LANES + lane)
    return places


def node_weights(places, nodes, half):
    lane = lanes()
    node = lane % 16
    landing = []
    for v in range(nodes // LANES):
        index = 32 * v + 4 * (lane // 16) + edge_of(node)
        picked = [jnp.take_along_axis(p, index, axis=1, mode="promise_in_bounds") for p in places]
        landing.append(jnp.where(odious(node), jnp.where(which_of(node) == 0, picked[0], picked[1]), -1)[0:1])
    landing = jnp.concatenate(landing, axis=1)
    row = lax.broadcasted_iota(jnp.int32, (3 * half, nodes), 0)
    return jnp.where(row == landing, 1.0, 0.0).astype(jnp.bfloat16)


def column_weights(places, nodes, half):
    lane = lanes()
    quarter = lane % 4

    def pick(t, edge):
        return jnp.take_along_axis(places[t], lane - quarter + edge, axis=1, mode="promise_in_bounds")

    def by_quarter(a, b, c, d):
        return jnp.where(quarter == 0, a, jnp.where(quarter == 1, b, jnp.where(quarter == 2, c, d)))[0:1]

    one = by_quarter(pick(0, 0), pick(1, 0), pick(0, 3), pick(1, 1))
    two = by_quarter(pick(1, 3), pick(0, 1), pick(1, 2), pick(0, 2))
    row = lax.broadcasted_iota(jnp.int32, (3 * half, LANES), 0)
    across = jnp.where((row == one) | (row == two), 0.125, 0.0).astype(jnp.bfloat16)
    row = lax.broadcasted_iota(jnp.int32, (nodes, LANES), 0)
    inner = row % 16
    column = 4 * (row // 16) + 2 * (inner // 8) + (inner % 4) // 2
    here = column == lax.broadcasted_iota(jnp.int32, (nodes, LANES), 1)
    own = jnp.where(here, jnp.where(odious(inner), 0.125, 0.25), 0.0).astype(jnp.bfloat16)
    return own, across


def first_kernel(
    devices, span, bounds, dyn_hbm, adj_hbm, cloud_hbm, source_hbm, sub_hbm,
    state, dsum_ref, count_ref, sums_e, profiles,
    dyn, adj, source_ref, sub_ref, edges, halo, outgoing, arrived, second, arrived2, sums_a, padded, bias, bias_a,
    local_sems, in_sems, halo_send, halo_recv, one_send, one_recv, two_send, two_recv,
):
    me = lax.axis_index("dev")
    groups = devices // GROUP
    group = me // GROUP
    member = me % GROUP
    above = (me + 1) % devices
    below = (me + devices - 1) % devices
    fields, levels, nodes = dyn.shape
    half = nodes // 2
    depth, width = state.shape[1], state.shape[2]
    parts = width // ROWS
    top = profiles.shape[1]

    barrier = pltpu.get_barrier_semaphore()

    def greet(device):
        pl.semaphore_signal(barrier, inc=1, device_id=(device,), device_id_type=pl.DeviceIdType.MESH)

    for step in range(1, groups):
        greet(((group + step) % groups) * GROUP + member)
    for step in range(1, GROUP):
        greet(group * GROUP + (member + step) % GROUP)
    greet(above)
    greet(below)

    local = []
    for i, (src, dst) in enumerate(((dyn_hbm, dyn), (source_hbm, source_ref), (sub_hbm, sub_ref), (adj_hbm, adj))):
        local.append(pltpu.make_async_copy(src, dst, local_sems.at[i]))
        local[-1].start()
    loads = []
    for i, (lo, hi) in enumerate(bounds):
        loads.append(pltpu.make_async_copy(cloud_hbm.at[:, lo:hi], state.at[:, lo:hi], in_sems.at[i]))
        loads[-1].start()

    local[0].wait()
    on_edge = odious(lanes((levels, LANES)) % 16)
    for f in range(fields):
        for j in range(2):
            first = dyn[f, :, 2 * j * LANES : (2 * j + 1) * LANES]
            later = dyn[f, :, (2 * j + 1) * LANES : (2 * j + 2) * LANES]
            edges[f, :, j * LANES : (j + 1) * LANES] = jnp.where(on_edge, first, pltpu.roll(later, 8, axis=1))

    local[1].wait()
    local[2].wait()
    slot = lanes((1, LANES))
    counts = jnp.zeros((1, LANES), jnp.int32)
    for i in range(LANES // span):
        counts = jnp.where(slot // span == i, sub_ref[0:1, i : i + 1], counts)
    source = source_ref[...]
    target = lax.broadcasted_iota(jnp.int32, (devices, LANES), 0)
    to_device = jnp.where(source // LANES == target, counts, 0).astype(jnp.float32).astype(jnp.bfloat16)
    row = lax.broadcasted_iota(jnp.int32, (LANES, LANES), 0)
    to_lane = jnp.where(source % LANES == row, 1.0, 0.0).astype(jnp.bfloat16)
    message = lax.dot_general(to_device, to_lane, (((1,), (1,)), ((), ())), preferred_element_type=jnp.float32)
    outgoing[...] = message.astype(jnp.int32).reshape(groups, GROUP, LANES)

    pl.semaphore_wait(barrier, groups - 1 + GROUP - 1 + 2)

    def send(src, dst, send_sem, recv_sem, device):
        copy = pltpu.make_async_remote_copy(
            src_ref=src, dst_ref=dst, send_sem=send_sem, recv_sem=recv_sem, device_id=(device,), device_id_type=pl.DeviceIdType.MESH
        )
        copy.start()
        return copy

    firsts = []
    for step in range(1, groups):
        to = (group + step) % groups
        firsts.append(send(outgoing.at[to], arrived.at[step], one_send.at[step], one_recv.at[step], to * GROUP + member))
    up = send(edges, halo.at[0], halo_send.at[0], halo_recv.at[0], above)
    down = send(edges, halo.at[1], halo_send.at[1], halo_recv.at[1], below)

    def begin(z, carry):
        all_a, all_e = [], []
        for k in range(parts):
            u0 = state[0, z, pl.ds(k, ROWS, stride=parts), :]
            u1 = state[1, z, pl.ds(k, ROWS, stride=parts), :]
            all_a.append(u0 + u1)
            all_e.append(u1 - 0.5 * u0)
        for k in range(parts):
            state[0, z, k * ROWS : (k + 1) * ROWS, :] = all_a[k]
            state[1, z, k * ROWS : (k + 1) * ROWS, :] = all_e[k]
        at = pl.multiple_of(z * ROWS, ROWS)
        sums_a[pl.ds(at, ROWS), :] = total_of(all_a)
        sums_e[pl.ds(at, ROWS), :] = total_of(all_e)
        return carry

    for (lo, hi), copy in zip(bounds, loads):
        copy.wait()
        lax.fori_loop(lo, hi, begin, 0)

    local[3].wait()
    places = partner_places(me, devices, adj, nodes // 16, half)
    own_weights, across_weights = column_weights(places, nodes, half)
    own = dyn[...].reshape(fields * levels, nodes)
    force_own = split_dot(own, own_weights)
    start_a = mean_of(sums_a, width)
    start_e = mean_of(sums_e, width)
    saturation = saturation_of(top, depth)
    bias_a[...] = -spread(padded, start_a, depth)

    for copy in firsts:
        copy.wait_recv()
    merged = outgoing[group]
    for step in range(1, groups):
        merged = merged + arrived[step]
    for q in range(GROUP):
        second[q] = jnp.broadcast_to(merged[q : q + 1, :], (ROWS, LANES))
    seconds = []
    for step in range(1, GROUP):
        to = (member + step) % GROUP
        seconds.append(send(second.at[to], arrived2.at[step], two_send.at[step], two_recv.at[step], group * GROUP + to))

    sweep(state, state, 0, None, bias_a, None, False, SHORT)
    weights = node_weights(places, nodes, half)

    up.wait()
    down.wait()
    values = [edges[...].reshape(fields * levels, half)] + [halo[i].reshape(fields * levels, half) for i in range(2)]
    values = jnp.concatenate(values, axis=1)
    force = force_own + split_dot(values, across_weights)
    force_0 = force[0:top]
    force_1 = force[levels : levels + top]
    force_e = force_1 - 0.5 * force_0
    force_a = force_0 + force_1
    bias[...] = spread(padded, 0.3 * (force_e - start_e), depth) - 10.0 * saturation
    sweep(state, state, 1, None, bias, sums_e, True, SHORT)

    profiles[0] = start_a
    profiles[1] = start_e
    profiles[2] = 0.3 * force_a
    profiles[3] = spread(padded, saturation + 0.3 * (force_e - saturation), depth) - 10.0 * saturation
    profiles[4] = 0.1 * spread(padded, 0.7 * start_a + 0.3 * force_a, depth)

    opposite = split_dot(values, weights)
    edge_lane = odious(lanes((fields * levels, nodes)) % 16)
    dsum_ref[...] = jnp.where(edge_lane, 0.5 * (own + opposite), own).reshape(fields, levels, nodes)

    for copy in seconds:
        copy.wait_recv()
    mine = second[member]
    for step in range(1, GROUP):
        mine = mine + arrived2[step]
    count_ref[...] = mine
    for copy in firsts + seconds:
        copy.wait_send()


def cut(depth):
    cuts = [round(i * depth / CHUNKS) for i in range(CHUNKS + 1)]
    return tuple(zip(cuts[:-1], cuts[1:]))


def first(dynamics, adjacency, cloud_state, span_source, substeps, devices):
    fields, levels, nodes = dynamics.shape
    depth, width = cloud_state.shape[1], cloud_state.shape[2]
    top = -(-depth // ROWS) * ROWS
    groups = devices // GROUP
    span = span_source.shape[0] // substeps.shape[0]
    vmem = pl.BlockSpec(memory_space=pltpu.VMEM)
    hbm = pl.BlockSpec(memory_space=pltpu.HBM)
    profile = pltpu.VMEM((top, LANES), jnp.float32)
    return pl.pallas_call(
        functools.partial(first_kernel, devices, span, cut(depth)),
        out_shape=(
            jax.ShapeDtypeStruct(cloud_state.shape, jnp.float32),
            jax.ShapeDtypeStruct(dynamics.shape, jnp.float32),
            jax.ShapeDtypeStruct((ROWS, LANES), jnp.int32),
            jax.ShapeDtypeStruct((top * ROWS, LANES), jnp.float32),
            jax.ShapeDtypeStruct((5, top, LANES), jnp.float32),
        ),
        in_specs=[hbm] * 5,
        out_specs=(vmem,) * 5,
        scratch_shapes=[
            pltpu.VMEM(dynamics.shape, jnp.float32),
            pltpu.VMEM(adjacency.shape, jnp.int32),
            pltpu.VMEM((1, LANES), jnp.int32),
            pltpu.VMEM((1, substeps.shape[0]), jnp.int32),
            pltpu.VMEM((fields, levels, nodes // 2), jnp.float32),
            pltpu.VMEM((2, fields, levels, nodes // 2), jnp.float32),
            pltpu.VMEM((groups, GROUP, LANES), jnp.int32),
            pltpu.VMEM((groups, GROUP, LANES), jnp.int32),
            pltpu.VMEM((GROUP, ROWS, LANES), jnp.int32),
            pltpu.VMEM((GROUP, ROWS, LANES), jnp.int32),
            pltpu.VMEM((top * ROWS, LANES), jnp.float32),
            pltpu.VMEM((top + 2 * PAD, LANES), jnp.float32),
            profile,
            profile,
            pltpu.SemaphoreType.DMA((4,)),
            pltpu.SemaphoreType.DMA((CHUNKS,)),
            pltpu.SemaphoreType.DMA((2,)),
            pltpu.SemaphoreType.DMA((2,)),
            pltpu.SemaphoreType.DMA((groups,)),
            pltpu.SemaphoreType.DMA((groups,)),
            pltpu.SemaphoreType.DMA((GROUP,)),
            pltpu.SemaphoreType.DMA((GROUP,)),
        ],
        compiler_params=pltpu.CompilerParams(collective_id=0, has_side_effects=True, vmem_limit_bytes=20 * 2**20),
        name="first",
    )(*[
        pltpu.with_memory_space_constraint(x, pltpu.HBM)
        for x in (dynamics, adjacency, cloud_state, span_source.reshape(1, -1), substeps.reshape(1, -1))
    ])


def rest_kernel(
    bounds, given, dsum_ref, count_ref, given_sums, profiles, dsum_out, tend_ref, new_ref,
    state, sums, mean_e, mean_a, bias, out_sems, dsum_sem,
):
    depth, width = state.shape[1], state.shape[2]
    parts = width // ROWS
    top = bias.shape[0]
    dsum_copy = pltpu.make_async_copy(dsum_ref, dsum_out, dsum_sem)
    dsum_copy.start()

    counts = count_ref[...]
    least = jnp.min(counts)
    most = jnp.max(counts)
    saturation = saturation_of(top, depth)

    def advance(scale, source_sums, active):
        bias[...] = scale * profiles[3] - 0.3 * spread(mean_e, mean_of(source_sums, width), depth)
        now = mean_a[PAD : PAD + top, :]
        later = 0.1 * spread(mean_a, 0.7 * now + profiles[2], depth)
        if active is not None:
            later = jnp.where(jnp.broadcast_to(active[0:1], (top, LANES)), later, now)
        mean_a[PAD : PAD + top, :] = later

    def plain(step, scale):
        advance(scale, sums, None)
        sweep(state, state, 0, None, None, None, False, UNROLL)
        sweep(state, state, 1, None, bias, sums, True, UNROLL)
        return scale * 10.0

    def masked(step, scale):
        active = counts > step
        advance(scale, sums, active)
        sweep(state, state, 0, active, None, None, False, UNROLL)
        sweep(state, state, 1, active, bias, sums, True, UNROLL)
        return scale * 10.0

    mean_a[PAD : PAD + top, :] = profiles[4]
    active = counts > 1
    advance(10.0, given_sums, active)
    sweep(given, state, 0, active, None, None, False, UNROLL)
    sweep(given, state, 1, active, bias, sums, True, UNROLL)
    middle = jnp.maximum(least, 2)
    scale = lax.fori_loop(2, middle, plain, jnp.float32(100.0))
    lax.fori_loop(middle, most, masked, scale)

    shrink = jnp.ones((ROWS, LANES), jnp.float32)
    for step in range(12):
        shrink = jnp.where(counts > step, shrink * 0.1, shrink)
    new_a = mean_a[PAD : PAD + top, :]
    new_e = mean_of(sums, width) * shrink[0:1] + saturation
    old_a = profiles[0]
    old_e = profiles[1]
    tend_0 = (2.0 / 3.0) * ((new_a - new_e) - (old_a - old_e))
    tend_1 = (new_a - old_a) - tend_0
    tend_ref[:, 0, :] = tend_0[0:depth]
    tend_ref[:, 1, :] = tend_1[0:depth]
    bias[...] = (2.0 / 3.0) * (new_a - saturation)
    shrink_0 = (2.0 / 3.0) * shrink

    def finish(z, carry):
        add_0 = jnp.broadcast_to(bias[pl.ds(z, 1), :], (ROWS, LANES))
        add_a = jnp.broadcast_to(mean_a[pl.ds(PAD + z, 1), :], (ROWS, LANES))
        new_0, new_1 = [], []
        for k in range(parts):
            a = state[0, z, k * ROWS : (k + 1) * ROWS, :]
            e = state[1, z, k * ROWS : (k + 1) * ROWS, :]
            u0 = (a - e) * shrink_0 + add_0
            new_0.append(u0)
            new_1.append((a * shrink + add_a) - u0)
        for k in range(parts):
            state[0, z, pl.ds(k, ROWS, stride=parts), :] = new_0[k]
            state[1, z, pl.ds(k, ROWS, stride=parts), :] = new_1[k]
        return carry

    stores = []
    for i, (lo, hi) in enumerate(bounds):
        lax.fori_loop(lo, hi, finish, 0, unroll=2)
        copy = pltpu.make_async_copy(state.at[:, lo:hi], new_ref.at[:, lo:hi], out_sems.at[i])
        copy.start()
        stores.append(copy)
    for copy in stores:
        copy.wait()
    dsum_copy.wait()


def rest(state, dsum, counts, sums, profiles):
    fields, depth, width, _ = state.shape
    top = profiles.shape[1]
    vmem = pl.BlockSpec(memory_space=pltpu.VMEM)
    hbm = pl.BlockSpec(memory_space=pltpu.HBM)
    padded = pltpu.VMEM((top + 2 * PAD, LANES), jnp.float32)
    return pl.pallas_call(
        functools.partial(rest_kernel, cut(depth)),
        out_shape=(
            jax.ShapeDtypeStruct(dsum.shape, jnp.float32),
            jax.ShapeDtypeStruct((depth, fields, LANES), jnp.float32),
            jax.ShapeDtypeStruct(state.shape, jnp.float32),
        ),
        in_specs=[vmem] * 5,
        out_specs=(hbm, vmem, hbm),
        scratch_shapes=[
            pltpu.VMEM(state.shape, jnp.float32),
            pltpu.VMEM(sums.shape, jnp.float32),
            padded,
            padded,
            pltpu.VMEM((top, LANES), jnp.float32),
            pltpu.SemaphoreType.DMA((CHUNKS,)),
            pltpu.SemaphoreType.DMA,
        ],
        compiler_params=pltpu.CompilerParams(vmem_limit_bytes=20 * 2**20),
        name="rest",
    )(state, dsum, counts, sums, profiles)


def on_device(dynamics, adjacency, cloud_state, span_source, substeps):
    devices = lax.axis_size("dev")
    carried = first(dynamics, adjacency, cloud_state, span_source, substeps, devices)
    dynamics_summed, tendency, cloud_new = rest(*carried)
    return dynamics_summed, jnp.transpose(tendency, (1, 0, 2)), cloud_new


def solution(mesh):
    in_specs = (
        P(None, None, "dev"),
        P(None, "dev"),
        P(None, None, None, "dev"),
        P("dev"),
        P("dev"),
    )
    out_specs = (P(None, None, "dev"), P(None, None, "dev"), P(None, None, None, "dev"))
    return jax.shard_map(on_device, mesh=mesh, in_specs=in_specs, out_specs=out_specs, check_vma=False)
```

time: 40.8 us -> 29.9 us (0.73)
  the two profiles are of different devices: /device:TPU:25 before, /device:TPU:9 now
where the time goes in v2:
time: 29.9 us; the launch traced here: 29.8 us
  Pallas kernels  29.1 us (97%)
  between operations  0.64 us (2%)
    pallas_call x1, Pallas kernels, first(): pl.pallas_call(functools.partial(first_kernel, devices, span, cut(depth))...  15.5 us
    pallas_call x1, Pallas kernels, rest(): pl.pallas_call(functools.partial(rest_kernel, cut(depth)), out_shape=(jax...  13.6 us

profile of v2, /device:TPU:9, one launch (start us, length us, event | category | flops | bytes accessed | tf_op | source)
XLA Modules:
  0.0 29.8 jit_solution(16179476351518210211)
XLA Ops:
  0.6 15.5 %first.1 = (f32[2,58,64,128]{3,2,1,0:T(8,128)S(1)}, f32[2,72,512]{2,1,0:T(8,128)S(1)}, s32[8,128]{1,0:T(8,128)S(1)}, f32[512,128]{1,0:T(8,128)S(1)}, f32[5,64,128]{2,1,0:T(8,128)S(1)}) custom-call(f32[2,72,512]{2,1,0:T(8,128)} %dyn_hbm.1, s32[2,128]{1,0:T(2,128)} %adj_hbm.1, f32[2,58,64,128]{3,2,1,0:T(8,128)} %cloud_hbm.1, s32[1,128]{1,0:T(1,128)} %bitcast.3, ...), custom_call_target="tpu_custom_call" | custom-call | tf_op jit(solution)/shard_map/first/pallas_call | solution.py:338
  16.1 13.6 %rest.1 = (f32[2,72,512]{2,1,0:T(8,128)}, f32[58,2,128]{2,1,0:T(2,128)}, f32[2,58,64,128]{3,2,1,0:T(8,128)}) custom-call(f32[2,58,64,128]{3,2,1,0:T(8,128)S(1)} %get-tuple-element.11.given, f32[2,72,512]{2,1,0:T(8,128)S(1)} %get-tuple-element.12.dsum_ref, s32[8,128]{1,0:T(8,128)S(1)} %get-tuple-element.13.count_ref, ...), custom_call_target="tpu_custom_call" | custom-call | tf_op jit(solution)/shard_map/rest/pallas_call | solution.py:472

commit v3 on v2

--- a/solution.py
+++ b/solution.py
@@ -9,11 +9,10 @@
 
 LANES = 128
 ROWS = 8
-GROUP = 8
 PAD = 8
 CHUNKS = 6
 UNROLL = 58
-SHORT = 2
+AHEAD = 6
 
 
 def odious(node):
@@ -133,56 +132,52 @@
     return places
 
 
-def node_weights(places, nodes, half):
-    lane = lanes()
-    node = lane % 16
+def packed_nodes(index):
+    lane = index % LANES
+    direct = odious(lane % 16)
+    moved = (lane + LANES - 8) % LANES
+    element = jnp.where(direct, lane // 16, 8 + moved // 16) + (index // LANES) * 16
+    return element, jnp.where(direct, lane % 16, moved % 16)
+
+
+def edge_weights(places, half):
     landing = []
-    for v in range(nodes // LANES):
-        index = 32 * v + 4 * (lane // 16) + edge_of(node)
+    for v in range(half // LANES):
+        element, node = packed_nodes(lanes() + v * LANES)
+        index = 4 * element + edge_of(node)
         picked = [jnp.take_along_axis(p, index, axis=1, mode="promise_in_bounds") for p in places]
-        landing.append(jnp.where(odious(node), jnp.where(which_of(node) == 0, picked[0], picked[1]), -1)[0:1])
+        landing.append(jnp.where(which_of(node) == 0, picked[0], picked[1])[0:1])
     landing = jnp.concatenate(landing, axis=1)
-    row = lax.broadcasted_iota(jnp.int32, (3 * half, nodes), 0)
+    row = lax.broadcasted_iota(jnp.int32, (3 * half, half), 0)
     return jnp.where(row == landing, 1.0, 0.0).astype(jnp.bfloat16)
 
 
-def column_weights(places, nodes, half):
-    lane = lanes()
-    quarter = lane % 4
-
-    def pick(t, edge):
-        return jnp.take_along_axis(places[t], lane - quarter + edge, axis=1, mode="promise_in_bounds")
-
-    def by_quarter(a, b, c, d):
-        return jnp.where(quarter == 0, a, jnp.where(quarter == 1, b, jnp.where(quarter == 2, c, d)))[0:1]
-
-    one = by_quarter(pick(0, 0), pick(1, 0), pick(0, 3), pick(1, 1))
-    two = by_quarter(pick(1, 3), pick(0, 1), pick(1, 2), pick(0, 2))
-    row = lax.broadcasted_iota(jnp.int32, (3 * half, LANES), 0)
-    across = jnp.where((row == one) | (row == two), 0.125, 0.0).astype(jnp.bfloat16)
-    row = lax.broadcasted_iota(jnp.int32, (nodes, LANES), 0)
-    inner = row % 16
-    column = 4 * (row // 16) + 2 * (inner // 8) + (inner % 4) // 2
-    here = column == lax.broadcasted_iota(jnp.int32, (nodes, LANES), 1)
-    own = jnp.where(here, jnp.where(odious(inner), 0.125, 0.25), 0.0).astype(jnp.bfloat16)
-    return own, across
+def quarter_weights(element, node, keep):
+    column = 4 * element + 2 * (node // 8) + (node % 4) // 2
+    here = (column == lax.broadcasted_iota(jnp.int32, column.shape, 1)) & keep
+    return jnp.where(here, 0.25, 0.0).astype(jnp.bfloat16)
 
 
 def first_kernel(
     devices, span, bounds, dyn_hbm, adj_hbm, cloud_hbm, source_hbm, sub_hbm,
-    state, dsum_ref, count_ref, sums_e, profiles,
-    dyn, adj, source_ref, sub_ref, edges, halo, outgoing, arrived, second, arrived2, sums_a, padded, bias, bias_a,
-    local_sems, in_sems, halo_send, halo_recv, one_send, one_recv, two_send, two_recv,
+    history, dsum_ref, count_ref, sums_e, mean_a, profiles,
+    loaded, dyn, adj, source_ref, sub_ref, edges, halo, outgoing, merged, arrived_y, arrived, sums, padded, bias, bias_a,
+    local_sems, in_sems, halo_send, halo_recv, leg_send, leg_recv,
 ):
     me = lax.axis_index("dev")
-    groups = devices // GROUP
-    group = me // GROUP
-    member = me % GROUP
+    strides = (devices // 4, devices // 16, devices // 64)
+    sibling = me + 1 - 2 * (me % 2)
     above = (me + 1) % devices
     below = (me + devices - 1) % devices
+
+    def along(stride, step):
+        at = (me // stride) % 4
+        to = (at + step) % 4
+        return to, me + (to - at) * stride
+
     fields, levels, nodes = dyn.shape
     half = nodes // 2
-    depth, width = state.shape[1], state.shape[2]
+    depth, width = loaded.shape[1], loaded.shape[2]
     parts = width // ROWS
     top = profiles.shape[1]
 
@@ -191,12 +186,12 @@
     def greet(device):
         pl.semaphore_signal(barrier, inc=1, device_id=(device,), device_id_type=pl.DeviceIdType.MESH)
 
-    for step in range(1, groups):
-        greet(((group + step) % groups) * GROUP + member)
-    for step in range(1, GROUP):
-        greet(group * GROUP + (member + step) % GROUP)
     greet(above)
     greet(below)
+    greet(sibling)
+    for stride in strides:
+        for step in range(1, 4):
+            greet(along(stride, step)[1])
 
     local = []
     for i, (src, dst) in enumerate(((dyn_hbm, dyn), (source_hbm, source_ref), (sub_hbm, sub_ref), (adj_hbm, adj))):
@@ -204,16 +199,16 @@
         local[-1].start()
     loads = []
     for i, (lo, hi) in enumerate(bounds):
-        loads.append(pltpu.make_async_copy(cloud_hbm.at[:, lo:hi], state.at[:, lo:hi], in_sems.at[i]))
+        loads.append(pltpu.make_async_copy(cloud_hbm.at[:, lo:hi], loaded.at[:, lo:hi], in_sems.at[i]))
         loads[-1].start()
 
     local[0].wait()
     on_edge = odious(lanes((levels, LANES)) % 16)
     for f in range(fields):
         for j in range(2):
-            first = dyn[f, :, 2 * j * LANES : (2 * j + 1) * LANES]
+            direct = dyn[f, :, 2 * j * LANES : (2 * j + 1) * LANES]
             later = dyn[f, :, (2 * j + 1) * LANES : (2 * j + 2) * LANES]
-            edges[f, :, j * LANES : (j + 1) * LANES] = jnp.where(on_edge, first, pltpu.roll(later, 8, axis=1))
+            edges[f, :, j * LANES : (j + 1) * LANES] = jnp.where(on_edge, direct, pltpu.roll(later, 8, axis=1))
 
     local[1].wait()
     local[2].wait()
@@ -227,9 +222,9 @@
     row = lax.broadcasted_iota(jnp.int32, (LANES, LANES), 0)
     to_lane = jnp.where(source % LANES == row, 1.0, 0.0).astype(jnp.bfloat16)
     message = lax.dot_general(to_device, to_lane, (((1,), (1,)), ((), ())), preferred_element_type=jnp.float32)
-    outgoing[...] = message.astype(jnp.int32).reshape(groups, GROUP, LANES)
-
-    pl.semaphore_wait(barrier, groups - 1 + GROUP - 1 + 2)
+    outgoing[...] = message.astype(jnp.int32).reshape(outgoing.shape)
+
+    pl.semaphore_wait(barrier, 12)
 
     def send(src, dst, send_sem, recv_sem, device):
         copy = pltpu.make_async_remote_copy(
@@ -238,86 +233,110 @@
         copy.start()
         return copy
 
-    firsts = []
-    for step in range(1, groups):
-        to = (group + step) % groups
-        firsts.append(send(outgoing.at[to], arrived.at[step], one_send.at[step], one_recv.at[step], to * GROUP + member))
+    rows_y = outgoing.shape[0] // 4
+    leg_y, leg_z, leg_x = [], [], []
+    for step in range(1, 4):
+        to, device = along(strides[0], step)
+        leg_y.append(send(outgoing.at[pl.ds(to * rows_y, rows_y)], arrived_y.at[step], leg_send.at[step], leg_recv.at[step], device))
     up = send(edges, halo.at[0], halo_send.at[0], halo_recv.at[0], above)
     down = send(edges, halo.at[1], halo_send.at[1], halo_recv.at[1], below)
 
     def begin(z, carry):
         all_a, all_e = [], []
         for k in range(parts):
-            u0 = state[0, z, pl.ds(k, ROWS, stride=parts), :]
-            u1 = state[1, z, pl.ds(k, ROWS, stride=parts), :]
+            u0 = loaded[0, z, pl.ds(k, ROWS, stride=parts), :]
+            u1 = loaded[1, z, pl.ds(k, ROWS, stride=parts), :]
             all_a.append(u0 + u1)
             all_e.append(u1 - 0.5 * u0)
         for k in range(parts):
-            state[0, z, k * ROWS : (k + 1) * ROWS, :] = all_a[k]
-            state[1, z, k * ROWS : (k + 1) * ROWS, :] = all_e[k]
+            loaded[0, z, k * ROWS : (k + 1) * ROWS, :] = all_a[k]
+            loaded[1, z, k * ROWS : (k + 1) * ROWS, :] = all_e[k]
         at = pl.multiple_of(z * ROWS, ROWS)
-        sums_a[pl.ds(at, ROWS), :] = total_of(all_a)
-        sums_e[pl.ds(at, ROWS), :] = total_of(all_e)
+        sums[0, pl.ds(at, ROWS), :] = total_of(all_a)
+        sums[1, pl.ds(at, ROWS), :] = total_of(all_e)
         return carry
 
     for (lo, hi), copy in zip(bounds, loads):
         copy.wait()
         lax.fori_loop(lo, hi, begin, 0)
 
-    local[3].wait()
-    places = partner_places(me, devices, adj, nodes // 16, half)
-    own_weights, across_weights = column_weights(places, nodes, half)
-    own = dyn[...].reshape(fields * levels, nodes)
-    force_own = split_dot(own, own_weights)
-    start_a = mean_of(sums_a, width)
-    start_e = mean_of(sums_e, width)
+    start_a = mean_of(sums.at[0], width)
+    start_e = mean_of(sums.at[1], width)
     saturation = saturation_of(top, depth)
     bias_a[...] = -spread(padded, start_a, depth)
-
-    for copy in firsts:
+    sweep(loaded, history.at[0], 0, None, bias_a, None, False, UNROLL)
+
+    local[3].wait()
+    weights = edge_weights(partner_places(me, devices, adj, nodes // 16, half), half)
+    row = lax.broadcasted_iota(jnp.int32, (nodes, LANES), 0)
+    own_weights = quarter_weights(row // 16, row % 16, ~odious(row % 16))
+    pool_weights = quarter_weights(*packed_nodes(lax.broadcasted_iota(jnp.int32, (half, LANES), 0)), True)
+    rows = fields * levels
+    force_own = split_dot(dyn[...].reshape(rows, nodes), own_weights)
+    own_edges = edges[...].reshape(rows, half)
+    opposite_own = split_dot(own_edges, weights[:half])
+
+    for copy in leg_y:
         copy.wait_recv()
-    merged = outgoing[group]
-    for step in range(1, groups):
-        merged = merged + arrived[step]
-    for q in range(GROUP):
-        second[q] = jnp.broadcast_to(merged[q : q + 1, :], (ROWS, LANES))
-    seconds = []
-    for step in range(1, GROUP):
-        to = (member + step) % GROUP
-        seconds.append(send(second.at[to], arrived2.at[step], two_send.at[step], two_recv.at[step], group * GROUP + to))
-
-    sweep(state, state, 0, None, bias_a, None, False, SHORT)
-    weights = node_weights(places, nodes, half)
+    at_y = (me // strides[0]) % 4
+    merged[...] = outgoing[pl.ds(at_y * rows_y, rows_y)] + arrived_y[1] + arrived_y[2] + arrived_y[3]
+    for step in range(1, 4):
+        to, device = along(strides[1], step)
+        leg_z.append(send(merged.at[to], arrived.at[step], leg_send.at[3 + step], leg_recv.at[3 + step], device))
 
     up.wait()
     down.wait()
-    values = [edges[...].reshape(fields * levels, half)] + [halo[i].reshape(fields * levels, half) for i in range(2)]
-    values = jnp.concatenate(values, axis=1)
-    force = force_own + split_dot(values, across_weights)
+    values = jnp.concatenate([halo[i].reshape(rows, half) for i in range(2)], axis=1)
+    averaged = 0.5 * (own_edges + (opposite_own + split_dot(values, weights[half:])))
+    force = force_own + split_dot(averaged, pool_weights)
     force_0 = force[0:top]
     force_1 = force[levels : levels + top]
     force_e = force_1 - 0.5 * force_0
     force_a = force_0 + force_1
     bias[...] = spread(padded, 0.3 * (force_e - start_e), depth) - 10.0 * saturation
-    sweep(state, state, 1, None, bias, sums_e, True, SHORT)
+    sweep(loaded, history.at[0], 1, None, bias, sums_e.at[0], True, UNROLL)
 
     profiles[0] = start_a
     profiles[1] = start_e
     profiles[2] = 0.3 * force_a
     profiles[3] = spread(padded, saturation + 0.3 * (force_e - saturation), depth) - 10.0 * saturation
-    profiles[4] = 0.1 * spread(padded, 0.7 * start_a + 0.3 * force_a, depth)
-
-    opposite = split_dot(values, weights)
-    edge_lane = odious(lanes((fields * levels, nodes)) % 16)
-    dsum_ref[...] = jnp.where(edge_lane, 0.5 * (own + opposite), own).reshape(fields, levels, nodes)
-
-    for copy in seconds:
+    mean_a[0] = 0.1 * spread(padded, 0.7 * start_a + 0.3 * force_a, depth)
+
+    def onward(step, scale):
+        before, after = history.at[step - 1], history.at[step]
+        bias[...] = scale * profiles[3] - 0.3 * spread(padded, mean_of(sums_e.at[step - 1], width), depth)
+        mean_a[step] = 0.1 * spread(padded, 0.7 * mean_a[step - 1] + profiles[2], depth)
+        sweep(before, after, 0, None, None, None, False, UNROLL)
+        sweep(before, after, 1, None, bias, sums_e.at[step], True, UNROLL)
+        return scale * 10.0
+
+    scale = lax.fori_loop(1, AHEAD // 3, onward, jnp.float32(10.0))
+
+    averaged = averaged.reshape(fields, levels, half)
+    for f in range(fields):
+        for j in range(2):
+            part = averaged[f, :, j * LANES : (j + 1) * LANES]
+            for v, moved in ((2 * j, part), (2 * j + 1, pltpu.roll(part, LANES - 8, axis=1))):
+                at = slice(v * LANES, (v + 1) * LANES)
+                dsum_ref[f, :, at] = jnp.where(on_edge, moved, dyn[f, :, at])
+
+    for copy in leg_z:
         copy.wait_recv()
-    mine = second[member]
-    for step in range(1, GROUP):
-        mine = mine + arrived2[step]
-    count_ref[...] = mine
-    for copy in firsts + seconds:
+    at_z = (me // strides[1]) % 4
+    arrived[0] = merged[at_z] + arrived[1] + arrived[2] + arrived[3]
+    for step in range(1, 4):
+        to, device = along(strides[2], step)
+        leg_x.append(send(arrived.at[0], arrived.at[3 + step], leg_send.at[6 + step], leg_recv.at[6 + step], device))
+    scale = lax.fori_loop(AHEAD // 3, 2 * AHEAD // 3, onward, scale)
+    for copy in leg_x:
+        copy.wait_recv()
+    arrived[7] = arrived[0] + arrived[4] + arrived[5] + arrived[6]
+    last = send(arrived.at[7], arrived.at[8], leg_send.at[0], leg_recv.at[0], sibling)
+    lax.fori_loop(2 * AHEAD // 3, AHEAD, onward, scale)
+    last.wait_recv()
+    member = pl.ds(me % ROWS, 1)
+    count_ref[...] = jnp.broadcast_to(arrived[7, member, :] + arrived[8, member, :], (ROWS, LANES))
+    for copy in leg_y + leg_z + leg_x + [last]:
         copy.wait_send()
 
 
@@ -330,7 +349,7 @@
     fields, levels, nodes = dynamics.shape
     depth, width = cloud_state.shape[1], cloud_state.shape[2]
     top = -(-depth // ROWS) * ROWS
-    groups = devices // GROUP
+    tiles = devices // ROWS
     span = span_source.shape[0] // substeps.shape[0]
     vmem = pl.BlockSpec(memory_space=pltpu.VMEM)
     hbm = pl.BlockSpec(memory_space=pltpu.HBM)
@@ -338,26 +357,28 @@
     return pl.pallas_call(
         functools.partial(first_kernel, devices, span, cut(depth)),
         out_shape=(
-            jax.ShapeDtypeStruct(cloud_state.shape, jnp.float32),
+            jax.ShapeDtypeStruct((AHEAD,) + cloud_state.shape, jnp.float32),
             jax.ShapeDtypeStruct(dynamics.shape, jnp.float32),
             jax.ShapeDtypeStruct((ROWS, LANES), jnp.int32),
-            jax.ShapeDtypeStruct((top * ROWS, LANES), jnp.float32),
-            jax.ShapeDtypeStruct((5, top, LANES), jnp.float32),
+            jax.ShapeDtypeStruct((AHEAD, top * ROWS, LANES), jnp.float32),
+            jax.ShapeDtypeStruct((AHEAD, top, LANES), jnp.float32),
+            jax.ShapeDtypeStruct((4, top, LANES), jnp.float32),
         ),
         in_specs=[hbm] * 5,
-        out_specs=(vmem,) * 5,
+        out_specs=(vmem,) * 6,
         scratch_shapes=[
+            pltpu.VMEM(cloud_state.shape, jnp.float32),
             pltpu.VMEM(dynamics.shape, jnp.float32),
             pltpu.VMEM(adjacency.shape, jnp.int32),
             pltpu.VMEM((1, LANES), jnp.int32),
             pltpu.VMEM((1, substeps.shape[0]), jnp.int32),
             pltpu.VMEM((fields, levels, nodes // 2), jnp.float32),
             pltpu.VMEM((2, fields, levels, nodes // 2), jnp.float32),
-            pltpu.VMEM((groups, GROUP, LANES), jnp.int32),
-            pltpu.VMEM((groups, GROUP, LANES), jnp.int32),
-            pltpu.VMEM((GROUP, ROWS, LANES), jnp.int32),
-            pltpu.VMEM((GROUP, ROWS, LANES), jnp.int32),
-            pltpu.VMEM((top * ROWS, LANES), jnp.float32),
+            pltpu.VMEM((tiles, ROWS, LANES), jnp.int32),
+            pltpu.VMEM((tiles // 4, ROWS, LANES), jnp.int32),
+            pltpu.VMEM((4, tiles // 4, ROWS, LANES), jnp.int32),
+            pltpu.VMEM((9, ROWS, LANES), jnp.int32),
+            pltpu.VMEM((2, top * ROWS, LANES), jnp.float32),
             pltpu.VMEM((top + 2 * PAD, LANES), jnp.float32),
             profile,
             profile,
@@ -365,12 +386,10 @@
             pltpu.SemaphoreType.DMA((CHUNKS,)),
             pltpu.SemaphoreType.DMA((2,)),
             pltpu.SemaphoreType.DMA((2,)),
-            pltpu.SemaphoreType.DMA((groups,)),
-            pltpu.SemaphoreType.DMA((groups,)),
-            pltpu.SemaphoreType.DMA((GROUP,)),
-            pltpu.SemaphoreType.DMA((GROUP,)),
+            pltpu.SemaphoreType.DMA((10,)),
+            pltpu.SemaphoreType.DMA((10,)),
         ],
-        compiler_params=pltpu.CompilerParams(collective_id=0, has_side_effects=True, vmem_limit_bytes=20 * 2**20),
+        compiler_params=pltpu.CompilerParams(collective_id=0, has_side_effects=True, vmem_limit_bytes=16 * 2**20),
         name="first",
     )(*[
         pltpu.with_memory_space_constraint(x, pltpu.HBM)
@@ -379,7 +398,7 @@
 
 
 def rest_kernel(
-    bounds, given, dsum_ref, count_ref, given_sums, profiles, dsum_out, tend_ref, new_ref,
+    bounds, history, dsum_ref, count_ref, sums_e, means_a, profiles, dsum_out, tend_ref, new_ref,
     state, sums, mean_e, mean_a, bias, out_sems, dsum_sem,
 ):
     depth, width = state.shape[1], state.shape[2]
@@ -414,13 +433,39 @@
         sweep(state, state, 1, active, bias, sums, True, UNROLL)
         return scale * 10.0
 
-    mean_a[PAD : PAD + top, :] = profiles[4]
-    active = counts > 1
-    advance(10.0, given_sums, active)
-    sweep(given, state, 0, active, None, None, False, UNROLL)
-    sweep(given, state, 1, active, bias, sums, True, UNROLL)
-    middle = jnp.maximum(least, 2)
-    scale = lax.fori_loop(2, middle, plain, jnp.float32(100.0))
+    @pl.when(least > AHEAD)
+    def _():
+        mean_a[PAD : PAD + top, :] = means_a[AHEAD - 1]
+        advance(10.0**AHEAD, sums_e.at[AHEAD - 1], None)
+        sweep(history.at[AHEAD - 1], state, 0, None, None, None, False, UNROLL)
+        sweep(history.at[AHEAD - 1], state, 1, None, bias, sums, True, UNROLL)
+
+    @pl.when(least <= AHEAD)
+    def _():
+        def pick(step, carry):
+            active = counts > step
+            row = active[0:1]
+
+            def level(z, carry):
+                for f in range(2):
+                    for k in range(parts):
+                        at = slice(k * ROWS, (k + 1) * ROWS)
+                        state[f, z, at, :] = jnp.where(active, history[step, f, z, at, :], state[f, z, at, :])
+                at = pl.ds(pl.multiple_of(z * ROWS, ROWS), ROWS)
+                sums[at, :] = jnp.where(active, sums_e[step, at, :], sums[at, :])
+                return carry
+
+            lax.fori_loop(0, depth, level, 0)
+            here = slice(PAD, PAD + top)
+            mean_a[here, :] = jnp.where(jnp.broadcast_to(row, (top, LANES)), means_a[step], mean_a[here, :])
+            return carry
+
+        lax.fori_loop(least - 1, jnp.minimum(most, AHEAD), pick, 0)
+
+    done = jnp.where(least > AHEAD, AHEAD + 1, AHEAD)
+    middle = jnp.maximum(least, done)
+    scale = jnp.where(least > AHEAD, jnp.float32(10.0 ** (AHEAD + 1)), jnp.float32(10.0**AHEAD))
+    scale = lax.fori_loop(done, middle, plain, scale)
     lax.fori_loop(middle, most, masked, scale)
 
     shrink = jnp.ones((ROWS, LANES), jnp.float32)
@@ -463,8 +508,8 @@
     dsum_copy.wait()
 
 
-def rest(state, dsum, counts, sums, profiles):
-    fields, depth, width, _ = state.shape
+def rest(history, dsum, counts, sums_e, means_a, profiles):
+    _, fields, depth, width, _ = history.shape
     top = profiles.shape[1]
     vmem = pl.BlockSpec(memory_space=pltpu.VMEM)
     hbm = pl.BlockSpec(memory_space=pltpu.HBM)
@@ -474,22 +519,22 @@
         out_shape=(
             jax.ShapeDtypeStruct(dsum.shape, jnp.float32),
             jax.ShapeDtypeStruct((depth, fields, LANES), jnp.float32),
-            jax.ShapeDtypeStruct(state.shape, jnp.float32),
+            jax.ShapeDtypeStruct(history.shape[1:], jnp.float32),
         ),
-        in_specs=[vmem] * 5,
+        in_specs=[vmem] * 6,
         out_specs=(hbm, vmem, hbm),
         scratch_shapes=[
-            pltpu.VMEM(state.shape, jnp.float32),
-            pltpu.VMEM(sums.shape, jnp.float32),
+            pltpu.VMEM(history.shape[1:], jnp.float32),
+            pltpu.VMEM(sums_e.shape[1:], jnp.float32),
             padded,
             padded,
             pltpu.VMEM((top, LANES), jnp.float32),
             pltpu.SemaphoreType.DMA((CHUNKS,)),
             pltpu.SemaphoreType.DMA,
         ],
-        compiler_params=pltpu.CompilerParams(vmem_limit_bytes=20 * 2**20),
+        compiler_params=pltpu.CompilerParams(vmem_limit_bytes=12 * 2**20),
         name="rest",
-    )(state, dsum, counts, sums, profiles)
+    )(history, dsum, counts, sums_e, means_a, profiles)
 
 
 def on_device(dynamics, adjacency, cloud_state, span_source, substeps):

time: 29.9 us -> 30.1 us (level)
  the two profiles are of different devices: /device:TPU:9 before, /device:TPU:0 now
where the time goes in v3:
time: 30.1 us; the launch traced here: 30 us
  Pallas kernels  29.4 us (98%)
  between operations  0.64 us (2%)
    pallas_call x1, Pallas kernels, first(): pl.pallas_call(functools.partial(first_kernel, devices, span, cut(depth))...  20.5 us
    pallas_call x1, Pallas kernels, rest(): pl.pallas_call(functools.partial(rest_kernel, cut(depth)), out_shape=(jax...  8.87 us

profile of v3, /device:TPU:0, one launch (start us, length us, event | category | flops | bytes accessed | tf_op | source)
XLA Modules:
  0.0 30.0 jit_solution(12654030716819396342)
XLA Ops:
  0.6 20.5 %first.1 = (f32[6,2,58,64,128]{4,3,2,1,0:T(8,128)S(1)}, f32[2,72,512]{2,1,0:T(8,128)S(1)}, s32[8,128]{1,0:T(8,128)S(1)}, f32[6,512,128]{2,1,0:T(8,128)S(1)}, f32...) custom-call(f32[2,72,512]{2,1,0:T(8,128)} %dyn_hbm.1, s32[2,128]{1,0:T(2,128)} %adj_hbm.1, ...), custom_call_target="tpu_custom_call" | custom-call | tf_op jit(solution)/shard_map/first/pallas_call | solution.py:357
  21.1 8.9 %rest.1 = (f32[2,72,512]{2,1,0:T(8,128)}, f32[58,2,128]{2,1,0:T(2,128)}, f32[2,58,64,128]{3,2,1,0:T(8,128)}) custom-call(f32[6,2,58,64,128]{4,3,2,1,0:T(8,128)S(1)} %get-tuple-element.12.history, f32[2,72,512]{2,1,0:T(8,128)S(1)} %get-tuple-element.13.dsum_ref, s32[8,128]{1,0:T(8,128)S(1)} %get-tuple-element.14.count_ref, ...), custom_call_target="tpu_custom_call" | custom-call | tf_op jit(solution)/shard_map/rest/pallas_call | solution.py:517

commit v4 on v3

--- a/solution.py
+++ b/solution.py
@@ -11,8 +11,8 @@
 ROWS = 8
 PAD = 8
 CHUNKS = 6
-UNROLL = 58
-AHEAD = 6
+AHEAD = 7
+READ_Z = 3
 
 
 def odious(node):
@@ -59,7 +59,7 @@
     return 0.8 * jnp.exp(-2.0 * height / depth)
 
 
-def sweep(src, dst, which, active, bias, sums, limit, unroll):
+def sweep(src, dst, which, active, bias, sums, limit, between=()):
     depth = src.shape[1]
     parts = src.shape[2] // ROWS
 
@@ -91,21 +91,46 @@
         return here, after
 
     before = here = load(0)
-    if unroll >= depth:
-        for z in range(depth):
-            before, here = level(z, before, here)
-        return
-    whole = depth // unroll
-
-    def several(i, carry):
-        before, here = carry
-        for j in range(unroll):
-            before, here = level(i * unroll + j, before, here)
-        return before, here
-
-    before, here = lax.fori_loop(0, whole, several, (before, here))
-    for z in range(whole * unroll, depth):
+    between = list(between)
+    for z in range(depth):
         before, here = level(z, before, here)
+        if between:
+            between.pop(0)()
+    for piece in between:
+        piece()
+
+
+def advance(scale, sums, terms, bias, pad_e, pad_a, now, later, width, depth, active=None):
+    top = bias.shape[0]
+    blocks = [(at, at + ROWS) for at in range(0, top, ROWS)]
+
+    def spread_of(pad, lo, hi):
+        return 8.0 * pad[PAD + lo : PAD + hi, :] + pad[PAD - 1 + lo : PAD - 1 + hi, :] + pad[PAD + 1 + lo : PAD + 1 + hi, :]
+
+    def ends(pad):
+        pad[PAD - 1 : PAD, :] = pad[PAD : PAD + 1, :]
+        pad[PAD + depth : PAD + depth + 1, :] = pad[PAD + depth - 1 : PAD + depth, :]
+
+    def mean_e(lo, hi):
+        rows = [sums[pl.ds(lo * ROWS + j, ROWS, stride=ROWS), :] for j in range(ROWS)]
+        pad_e[PAD + lo : PAD + hi, :] = total_of(rows) * (1.0 / width)
+
+    def bias_e(lo, hi):
+        bias[lo:hi, :] = scale * terms[3, lo:hi, :] - 0.3 * spread_of(pad_e, lo, hi)
+
+    def relaxed_a(lo, hi):
+        pad_a[PAD + lo : PAD + hi, :] = 0.7 * now[lo:hi, :] + terms[2, lo:hi, :]
+
+    def mean_a(lo, hi):
+        value = 0.1 * spread_of(pad_a, lo, hi)
+        if active is not None:
+            value = jnp.where(active, value, now[lo:hi, :])
+        later[lo:hi, :] = value
+
+    pieces = [functools.partial(mean_e, *block) for block in blocks] + [functools.partial(ends, pad_e)]
+    pieces += [functools.partial(bias_e, *block) for block in blocks]
+    pieces += [functools.partial(relaxed_a, *block) for block in blocks] + [functools.partial(ends, pad_a)]
+    return pieces + [functools.partial(mean_a, *block) for block in blocks]
 
 
 def split_dot(values, weights):
@@ -161,12 +186,13 @@
 def first_kernel(
     devices, span, bounds, dyn_hbm, adj_hbm, cloud_hbm, source_hbm, sub_hbm,
     history, dsum_ref, count_ref, sums_e, mean_a, profiles,
-    loaded, dyn, adj, source_ref, sub_ref, edges, halo, outgoing, merged, arrived_y, arrived, sums, padded, bias, bias_a,
+    loaded, dyn, adj, source_ref, sub_ref, edges, halo, outgoing, merged, arrived_y, arrived_z, arrived_x,
+    sums, padded, padded_a, bias, bias_a,
     local_sems, in_sems, halo_send, halo_recv, leg_send, leg_recv,
 ):
     me = lax.axis_index("dev")
-    strides = (devices // 4, devices // 16, devices // 64)
-    sibling = me + 1 - 2 * (me % 2)
+    strides = (devices // 4, devices // 16)
+    member = me % ROWS
     above = (me + 1) % devices
     below = (me + devices - 1) % devices
 
@@ -188,10 +214,11 @@
 
     greet(above)
     greet(below)
-    greet(sibling)
     for stride in strides:
         for step in range(1, 4):
             greet(along(stride, step)[1])
+    for step in range(1, ROWS):
+        greet(me - member + (member + step) % ROWS)
 
     local = []
     for i, (src, dst) in enumerate(((dyn_hbm, dyn), (source_hbm, source_ref), (sub_hbm, sub_ref), (adj_hbm, adj))):
@@ -224,7 +251,7 @@
     message = lax.dot_general(to_device, to_lane, (((1,), (1,)), ((), ())), preferred_element_type=jnp.float32)
     outgoing[...] = message.astype(jnp.int32).reshape(outgoing.shape)
 
-    pl.semaphore_wait(barrier, 12)
+    pl.semaphore_wait(barrier, 2 + 3 + 3 + ROWS - 1)
 
     def send(src, dst, send_sem, recv_sem, device):
         copy = pltpu.make_async_remote_copy(
@@ -264,7 +291,7 @@
     start_e = mean_of(sums.at[1], width)
     saturation = saturation_of(top, depth)
     bias_a[...] = -spread(padded, start_a, depth)
-    sweep(loaded, history.at[0], 0, None, bias_a, None, False, UNROLL)
+    sweep(loaded, history.at[0], 0, None, bias_a, None, False)
 
     local[3].wait()
     weights = edge_weights(partner_places(me, devices, adj, nodes // 16, half), half)
@@ -282,7 +309,7 @@
     merged[...] = outgoing[pl.ds(at_y * rows_y, rows_y)] + arrived_y[1] + arrived_y[2] + arrived_y[3]
     for step in range(1, 4):
         to, device = along(strides[1], step)
-        leg_z.append(send(merged.at[to], arrived.at[step], leg_send.at[3 + step], leg_recv.at[3 + step], device))
+        leg_z.append(send(merged.at[to], arrived_z.at[step], leg_send.at[3 + step], leg_recv.at[3 + step], device))
 
     up.wait()
     down.wait()
@@ -294,7 +321,7 @@
     force_e = force_1 - 0.5 * force_0
     force_a = force_0 + force_1
     bias[...] = spread(padded, 0.3 * (force_e - start_e), depth) - 10.0 * saturation
-    sweep(loaded, history.at[0], 1, None, bias, sums_e.at[0], True, UNROLL)
+    sweep(loaded, history.at[0], 1, None, bias, sums_e.at[0], True)
 
     profiles[0] = start_a
     profiles[1] = start_e
@@ -304,13 +331,22 @@
 
     def onward(step, scale):
         before, after = history.at[step - 1], history.at[step]
-        bias[...] = scale * profiles[3] - 0.3 * spread(padded, mean_of(sums_e.at[step - 1], width), depth)
-        mean_a[step] = 0.1 * spread(padded, 0.7 * mean_a[step - 1] + profiles[2], depth)
-        sweep(before, after, 0, None, None, None, False, UNROLL)
-        sweep(before, after, 1, None, bias, sums_e.at[step], True, UNROLL)
+        pieces = advance(
+            scale, sums_e.at[step - 1], profiles, bias, padded, padded_a, mean_a.at[step - 1], mean_a.at[step], width, depth
+        )
+        sweep(before, after, 0, None, None, None, False, pieces)
+        sweep(before, after, 1, None, bias, sums_e.at[step], True)
         return scale * 10.0
 
-    scale = lax.fori_loop(1, AHEAD // 3, onward, jnp.float32(10.0))
+    scale = lax.fori_loop(1, READ_Z, onward, jnp.float32(10.0))
+    for copy in leg_z:
+        copy.wait_recv()
+    at_z = (me // strides[1]) % 4
+    arrived_x[0] = merged[at_z] + arrived_z[1] + arrived_z[2] + arrived_z[3]
+    for step in range(1, ROWS):
+        device = me - member + (member + step) % ROWS
+        leg_x.append(send(arrived_x.at[0], arrived_x.at[step], leg_send.at[6 + step], leg_recv.at[6 + step], device))
+    lax.fori_loop(READ_Z, AHEAD, onward, scale)
 
     averaged = averaged.reshape(fields, levels, half)
     for f in range(fields):
@@ -320,23 +356,11 @@
                 at = slice(v * LANES, (v + 1) * LANES)
                 dsum_ref[f, :, at] = jnp.where(on_edge, moved, dyn[f, :, at])
 
-    for copy in leg_z:
-        copy.wait_recv()
-    at_z = (me // strides[1]) % 4
-    arrived[0] = merged[at_z] + arrived[1] + arrived[2] + arrived[3]
-    for step in range(1, 4):
-        to, device = along(strides[2], step)
-        leg_x.append(send(arrived.at[0], arrived.at[3 + step], leg_send.at[6 + step], leg_recv.at[6 + step], device))
-    scale = lax.fori_loop(AHEAD // 3, 2 * AHEAD // 3, onward, scale)
     for copy in leg_x:
         copy.wait_recv()
-    arrived[7] = arrived[0] + arrived[4] + arrived[5] + arrived[6]
-    last = send(arrived.at[7], arrived.at[8], leg_send.at[0], leg_recv.at[0], sibling)
-    lax.fori_loop(2 * AHEAD // 3, AHEAD, onward, scale)
-    last.wait_recv()
-    member = pl.ds(me % ROWS, 1)
-    count_ref[...] = jnp.broadcast_to(arrived[7, member, :] + arrived[8, member, :], (ROWS, LANES))
-    for copy in leg_y + leg_z + leg_x + [last]:
+    mine = total_of([arrived_x[i, pl.ds(member, 1), :] for i in range(ROWS)])
+    count_ref[...] = jnp.broadcast_to(mine, (ROWS, LANES))
+    for copy in leg_y + leg_z + leg_x:
         copy.wait_send()
 
 
@@ -377,8 +401,10 @@
             pltpu.VMEM((tiles, ROWS, LANES), jnp.int32),
             pltpu.VMEM((tiles // 4, ROWS, LANES), jnp.int32),
             pltpu.VMEM((4, tiles // 4, ROWS, LANES), jnp.int32),
-            pltpu.VMEM((9, ROWS, LANES), jnp.int32),
+            pltpu.VMEM((4, ROWS, LANES), jnp.int32),
+            pltpu.VMEM((ROWS, ROWS, LANES), jnp.int32),
             pltpu.VMEM((2, top * ROWS, LANES), jnp.float32),
+            pltpu.VMEM((top + 2 * PAD, LANES), jnp.float32),
             pltpu.VMEM((top + 2 * PAD, LANES), jnp.float32),
             profile,
             profile,
@@ -386,10 +412,10 @@
             pltpu.SemaphoreType.DMA((CHUNKS,)),
             pltpu.SemaphoreType.DMA((2,)),
             pltpu.SemaphoreType.DMA((2,)),
-            pltpu.SemaphoreType.DMA((10,)),
-            pltpu.SemaphoreType.DMA((10,)),
+            pltpu.SemaphoreType.DMA((14,)),
+            pltpu.SemaphoreType.DMA((14,)),
         ],
-        compiler_params=pltpu.CompilerParams(collective_id=0, has_side_effects=True, vmem_limit_bytes=16 * 2**20),
+        compiler_params=pltpu.CompilerParams(collective_id=0, has_side_effects=True, vmem_limit_bytes=10 * 2**20),
         name="first",
     )(*[
         pltpu.with_memory_space_constraint(x, pltpu.HBM)
@@ -399,7 +425,7 @@
 
 def rest_kernel(
     bounds, history, dsum_ref, count_ref, sums_e, means_a, profiles, dsum_out, tend_ref, new_ref,
-    state, sums, mean_e, mean_a, bias, out_sems, dsum_sem,
+    state, sums, padded, padded_a, mean_a, bias, out_sems, dsum_sem,
 ):
     depth, width = state.shape[1], state.shape[2]
     parts = width // ROWS
@@ -412,39 +438,27 @@
     most = jnp.max(counts)
     saturation = saturation_of(top, depth)
 
-    def advance(scale, source_sums, active):
-        bias[...] = scale * profiles[3] - 0.3 * spread(mean_e, mean_of(source_sums, width), depth)
-        now = mean_a[PAD : PAD + top, :]
-        later = 0.1 * spread(mean_a, 0.7 * now + profiles[2], depth)
-        if active is not None:
-            later = jnp.where(jnp.broadcast_to(active[0:1], (top, LANES)), later, now)
-        mean_a[PAD : PAD + top, :] = later
+    def substep(src, source_sums, source_mean, scale, active):
+        pieces = advance(scale, source_sums, profiles, bias, padded, padded_a, source_mean, mean_a, width, depth, active)
+        sweep(src, state, 0, active, None, None, False, pieces)
+        sweep(src, state, 1, active, bias, sums, True)
+        return scale * 10.0
 
     def plain(step, scale):
-        advance(scale, sums, None)
-        sweep(state, state, 0, None, None, None, False, UNROLL)
-        sweep(state, state, 1, None, bias, sums, True, UNROLL)
-        return scale * 10.0
+        return substep(state, sums, mean_a, scale, None)
 
     def masked(step, scale):
-        active = counts > step
-        advance(scale, sums, active)
-        sweep(state, state, 0, active, None, None, False, UNROLL)
-        sweep(state, state, 1, active, bias, sums, True, UNROLL)
-        return scale * 10.0
+        return substep(state, sums, mean_a, scale, counts > step)
 
     @pl.when(least > AHEAD)
     def _():
-        mean_a[PAD : PAD + top, :] = means_a[AHEAD - 1]
-        advance(10.0**AHEAD, sums_e.at[AHEAD - 1], None)
-        sweep(history.at[AHEAD - 1], state, 0, None, None, None, False, UNROLL)
-        sweep(history.at[AHEAD - 1], state, 1, None, bias, sums, True, UNROLL)
+        last = AHEAD - 1
+        substep(history.at[last], sums_e.at[last], means_a.at[last], 10.0**AHEAD, None)
 
     @pl.when(least <= AHEAD)
     def _():
         def pick(step, carry):
             active = counts > step
-            row = active[0:1]
 
             def level(z, carry):
                 for f in range(2):
@@ -456,8 +470,7 @@
                 return carry
 
             lax.fori_loop(0, depth, level, 0)
-            here = slice(PAD, PAD + top)
-            mean_a[here, :] = jnp.where(jnp.broadcast_to(row, (top, LANES)), means_a[step], mean_a[here, :])
+            mean_a[...] = jnp.where(jnp.broadcast_to(active[0:1], (top, LANES)), means_a[step], mean_a[...])
             return carry
 
         lax.fori_loop(least - 1, jnp.minimum(most, AHEAD), pick, 0)
@@ -471,7 +484,7 @@
     shrink = jnp.ones((ROWS, LANES), jnp.float32)
     for step in range(12):
         shrink = jnp.where(counts > step, shrink * 0.1, shrink)
-    new_a = mean_a[PAD : PAD + top, :]
+    new_a = mean_a[...]
     new_e = mean_of(sums, width) * shrink[0:1] + saturation
     old_a = profiles[0]
     old_e = profiles[1]
@@ -482,9 +495,9 @@
     bias[...] = (2.0 / 3.0) * (new_a - saturation)
     shrink_0 = (2.0 / 3.0) * shrink
 
-    def finish(z, carry):
+    def finish(z):
         add_0 = jnp.broadcast_to(bias[pl.ds(z, 1), :], (ROWS, LANES))
-        add_a = jnp.broadcast_to(mean_a[pl.ds(PAD + z, 1), :], (ROWS, LANES))
+        add_a = jnp.broadcast_to(mean_a[pl.ds(z, 1), :], (ROWS, LANES))
         new_0, new_1 = [], []
         for k in range(parts):
             a = state[0, z, k * ROWS : (k + 1) * ROWS, :]
@@ -495,11 +508,11 @@
         for k in range(parts):
             state[0, z, pl.ds(k, ROWS, stride=parts), :] = new_0[k]
             state[1, z, pl.ds(k, ROWS, stride=parts), :] = new_1[k]
-        return carry
 
     stores = []
     for i, (lo, hi) in enumerate(bounds):
-        lax.fori_loop(lo, hi, finish, 0, unroll=2)
+        for z in range(lo, hi):
+            finish(z)
         copy = pltpu.make_async_copy(state.at[:, lo:hi], new_ref.at[:, lo:hi], out_sems.at[i])
         copy.start()
         stores.append(copy)
@@ -529,10 +542,11 @@
             padded,
             padded,
             pltpu.VMEM((top, LANES), jnp.float32),
+            pltpu.VMEM((top, LANES), jnp.float32),
             pltpu.SemaphoreType.DMA((CHUNKS,)),
             pltpu.SemaphoreType.DMA,
         ],
-        compiler_params=pltpu.CompilerParams(vmem_limit_bytes=12 * 2**20),
+        compiler_params=pltpu.CompilerParams(vmem_limit_bytes=8 * 2**20),
         name="rest",
     )(history, dsum, counts, sums_e, means_a, profiles)
 

time: 30.1 us -> 26.5 us (0.88)
  Pallas kernels: 29.4 us -> 25.7 us
    pallas_call x1, Pallas kernels: 8.87 us -> 4.14 us  [rest(): pl.pallas_call(functools.partial(rest_kernel, cut(depth)), out_shape=(jax...]
    pallas_call x1, Pallas kernels: 20.5 us -> 21.6 us  [first(): pl.pallas_call(functools.partial(first_kernel, devices, span, cut(depth))...]
where the time goes in v4:
time: 26.5 us; the launch traced here: 26.4 us
  Pallas kernels  25.7 us (97%)
  between operations  0.64 us (2%)
    pallas_call x1, Pallas kernels, first(): pl.pallas_call(functools.partial(first_kernel, devices, span, cut(depth))...  21.6 us
    pallas_call x1, Pallas kernels, rest(): pl.pallas_call(functools.partial(rest_kernel, cut(depth)), out_shape=(jax...  4.14 us

profile of v4, /device:TPU:0, one launch (start us, length us, event | category | flops | bytes accessed | tf_op | source)
XLA Modules:
  0.0 26.4 jit_solution(1674376750955685892)
XLA Ops:
  0.6 21.6 %first.1 = (f32[7,2,58,64,128]{4,3,2,1,0:T(8,128)S(1)}, f32[2,72,512]{2,1,0:T(8,128)S(1)}, s32[8,128]{1,0:T(8,128)S(1)}, f32[7,512,128]{2,1,0:T(8,128)S(1)}, f32...) custom-call(f32[2,72,512]{2,1,0:T(8,128)} %dyn_hbm.1, s32[2,128]{1,0:T(2,128)} %adj_hbm.1, ...), custom_call_target="tpu_custom_call" | custom-call | tf_op jit(solution)/shard_map/first/pallas_call | solution.py:381
  22.2 4.1 %rest.1 = (f32[2,72,512]{2,1,0:T(8,128)}, f32[58,2,128]{2,1,0:T(2,128)}, f32[2,58,64,128]{3,2,1,0:T(8,128)}) custom-call(f32[7,2,58,64,128]{4,3,2,1,0:T(8,128)S(1)} %get-tuple-element.12.history, f32[2,72,512]{2,1,0:T(8,128)S(1)} %get-tuple-element.13.dsum_ref, s32[8,128]{1,0:T(8,128)S(1)} %get-tuple-element.14.count_ref, ...), custom_call_target="tpu_custom_call" | custom-call | tf_op jit(solution)/shard_map/rest/pallas_call | solution.py:530

commit v5 on v4

--- a/solution.py
+++ b/solution.py
@@ -12,7 +12,6 @@
 PAD = 8
 CHUNKS = 6
 AHEAD = 7
-READ_Z = 3
 
 
 def odious(node):
@@ -59,7 +58,7 @@
     return 0.8 * jnp.exp(-2.0 * height / depth)
 
 
-def sweep(src, dst, which, active, bias, sums, limit, between=()):
+def sweep(src, dst, which, active, bias, sums, limit, between=(), emit=None):
     depth = src.shape[1]
     parts = src.shape[2] // ROWS
 
@@ -67,12 +66,11 @@
         return [src[which, z, k * ROWS : (k + 1) * ROWS, :] for k in range(parts)]
 
     def level(z, before, here):
-        known = isinstance(z, int)
-        after = load(min(z + 1, depth - 1) if known else jnp.minimum(z + 1, depth - 1))
+        after = load(min(z + 1, depth - 1))
         left = pltpu.roll(here[parts - 1], 1, axis=0)
         right = pltpu.roll(here[0], ROWS - 1, axis=0)
         if bias is not None:
-            shift = jnp.broadcast_to(bias[pl.ds(z, 1), :], (ROWS, LANES))
+            shift = jnp.broadcast_to(bias[z : z + 1, :], (ROWS, LANES))
         stepped = []
         for k in range(parts):
             beside = (here[k - 1] if k > 0 else left) + (here[k + 1] if k < parts - 1 else right)
@@ -84,10 +82,12 @@
             if active is not None:
                 value = jnp.where(active, value, here[k])
             stepped.append(value)
-            dst[which, z, k * ROWS : (k + 1) * ROWS, :] = value
+            if emit is None:
+                dst[which, z, k * ROWS : (k + 1) * ROWS, :] = value
+        if emit is not None:
+            emit(z, stepped)
         if sums is not None:
-            at = z * ROWS if known else pl.multiple_of(z * ROWS, ROWS)
-            sums[pl.ds(at, ROWS), :] = total_of(stepped)
+            sums[z * ROWS : (z + 1) * ROWS, :] = total_of(stepped)
         return here, after
 
     before = here = load(0)
@@ -185,7 +185,7 @@
 
 def first_kernel(
     devices, span, bounds, dyn_hbm, adj_hbm, cloud_hbm, source_hbm, sub_hbm,
-    history, dsum_ref, count_ref, sums_e, mean_a, profiles,
+    early, state, dsum_ref, count_ref, sums_e, mean_a, profiles,
     loaded, dyn, adj, source_ref, sub_ref, edges, halo, outgoing, merged, arrived_y, arrived_z, arrived_x,
     sums, padded, padded_a, bias, bias_a,
     local_sems, in_sems, halo_send, halo_recv, leg_send, leg_recv,
@@ -267,6 +267,16 @@
         leg_y.append(send(outgoing.at[pl.ds(to * rows_y, rows_y)], arrived_y.at[step], leg_send.at[step], leg_recv.at[step], device))
     up = send(edges, halo.at[0], halo_send.at[0], halo_recv.at[0], above)
     down = send(edges, halo.at[1], halo_send.at[1], halo_recv.at[1], below)
+
+    local[3].wait()
+    weights = edge_weights(partner_places(me, devices, adj, nodes // 16, half), half)
+    row = lax.broadcasted_iota(jnp.int32, (nodes, LANES), 0)
+    own_weights = quarter_weights(row // 16, row % 16, ~odious(row % 16))
+    pool_weights = quarter_weights(*packed_nodes(lax.broadcasted_iota(jnp.int32, (half, LANES), 0)), True)
+    rows = fields * levels
+    force_own = split_dot(dyn[...].reshape(rows, nodes), own_weights)
+    own_edges = edges[...].reshape(rows, half)
+    opposite_own = split_dot(own_edges, weights[:half])
 
     def begin(z, carry):
         all_a, all_e = [], []
@@ -285,23 +295,13 @@
 
     for (lo, hi), copy in zip(bounds, loads):
         copy.wait()
-        lax.fori_loop(lo, hi, begin, 0)
+        lax.fori_loop(lo, hi, begin, 0, unroll=2)
 
     start_a = mean_of(sums.at[0], width)
     start_e = mean_of(sums.at[1], width)
     saturation = saturation_of(top, depth)
     bias_a[...] = -spread(padded, start_a, depth)
-    sweep(loaded, history.at[0], 0, None, bias_a, None, False)
-
-    local[3].wait()
-    weights = edge_weights(partner_places(me, devices, adj, nodes // 16, half), half)
-    row = lax.broadcasted_iota(jnp.int32, (nodes, LANES), 0)
-    own_weights = quarter_weights(row // 16, row % 16, ~odious(row % 16))
-    pool_weights = quarter_weights(*packed_nodes(lax.broadcasted_iota(jnp.int32, (half, LANES), 0)), True)
-    rows = fields * levels
-    force_own = split_dot(dyn[...].reshape(rows, nodes), own_weights)
-    own_edges = edges[...].reshape(rows, half)
-    opposite_own = split_dot(own_edges, weights[:half])
+    sweep(loaded, early, 0, None, bias_a, None, False)
 
     for copy in leg_y:
         copy.wait_recv()
@@ -321,7 +321,7 @@
     force_e = force_1 - 0.5 * force_0
     force_a = force_0 + force_1
     bias[...] = spread(padded, 0.3 * (force_e - start_e), depth) - 10.0 * saturation
-    sweep(loaded, history.at[0], 1, None, bias, sums_e.at[0], True)
+    sweep(loaded, early, 1, None, bias, sums_e.at[0], True)
 
     profiles[0] = start_a
     profiles[1] = start_e
@@ -329,16 +329,15 @@
     profiles[3] = spread(padded, saturation + 0.3 * (force_e - saturation), depth) - 10.0 * saturation
     mean_a[0] = 0.1 * spread(padded, 0.7 * start_a + 0.3 * force_a, depth)
 
-    def onward(step, scale):
-        before, after = history.at[step - 1], history.at[step]
+    def onward(source, before, scale):
         pieces = advance(
-            scale, sums_e.at[step - 1], profiles, bias, padded, padded_a, mean_a.at[step - 1], mean_a.at[step], width, depth
+            scale, sums_e.at[before], profiles, bias, padded, padded_a, mean_a.at[before], mean_a.at[1], width, depth
         )
-        sweep(before, after, 0, None, None, None, False, pieces)
-        sweep(before, after, 1, None, bias, sums_e.at[step], True)
+        sweep(source, state, 0, None, None, None, False, pieces)
+        sweep(source, state, 1, None, bias, sums_e.at[1], True)
         return scale * 10.0
 
-    scale = lax.fori_loop(1, READ_Z, onward, jnp.float32(10.0))
+    onward(early, 0, 10.0)
     for copy in leg_z:
         copy.wait_recv()
     at_z = (me // strides[1]) % 4
@@ -346,7 +345,7 @@
     for step in range(1, ROWS):
         device = me - member + (member + step) % ROWS
         leg_x.append(send(arrived_x.at[0], arrived_x.at[step], leg_send.at[6 + step], leg_recv.at[6 + step], device))
-    lax.fori_loop(READ_Z, AHEAD, onward, scale)
+    lax.fori_loop(2, AHEAD, lambda step, scale: onward(state, 1, scale), jnp.float32(100.0))
 
     averaged = averaged.reshape(fields, levels, half)
     for f in range(fields):
@@ -381,15 +380,16 @@
     return pl.pallas_call(
         functools.partial(first_kernel, devices, span, cut(depth)),
         out_shape=(
-            jax.ShapeDtypeStruct((AHEAD,) + cloud_state.shape, jnp.float32),
+            jax.ShapeDtypeStruct(cloud_state.shape, jnp.float32),
+            jax.ShapeDtypeStruct(cloud_state.shape, jnp.float32),
             jax.ShapeDtypeStruct(dynamics.shape, jnp.float32),
             jax.ShapeDtypeStruct((ROWS, LANES), jnp.int32),
-            jax.ShapeDtypeStruct((AHEAD, top * ROWS, LANES), jnp.float32),
-            jax.ShapeDtypeStruct((AHEAD, top, LANES), jnp.float32),
+            jax.ShapeDtypeStruct((2, top * ROWS, LANES), jnp.float32),
+            jax.ShapeDtypeStruct((2, top, LANES), jnp.float32),
             jax.ShapeDtypeStruct((4, top, LANES), jnp.float32),
         ),
         in_specs=[hbm] * 5,
-        out_specs=(vmem,) * 6,
+        out_specs=(vmem,) * 7,
         scratch_shapes=[
             pltpu.VMEM(cloud_state.shape, jnp.float32),
             pltpu.VMEM(dynamics.shape, jnp.float32),
@@ -424,8 +424,8 @@
 
 
 def rest_kernel(
-    bounds, history, dsum_ref, count_ref, sums_e, means_a, profiles, dsum_out, tend_ref, new_ref,
-    state, sums, padded, padded_a, mean_a, bias, out_sems, dsum_sem,
+    bounds, early, ahead, dsum_ref, count_ref, sums_e, means_a, profiles, dsum_out, tend_ref, new_ref,
+    state, sums, padded, padded_a, mean_a, bias, add, out_sems, dsum_sem,
 ):
     depth, width = state.shape[1], state.shape[2]
     parts = width // ROWS
@@ -452,38 +452,58 @@
 
     @pl.when(least > AHEAD)
     def _():
-        last = AHEAD - 1
-        substep(history.at[last], sums_e.at[last], means_a.at[last], 10.0**AHEAD, None)
+        substep(ahead, sums_e.at[1], means_a.at[1], 10.0**AHEAD, None)
 
     @pl.when(least <= AHEAD)
     def _():
-        def pick(step, carry):
-            active = counts > step
-
-            def level(z, carry):
-                for f in range(2):
-                    for k in range(parts):
-                        at = slice(k * ROWS, (k + 1) * ROWS)
-                        state[f, z, at, :] = jnp.where(active, history[step, f, z, at, :], state[f, z, at, :])
-                at = pl.ds(pl.multiple_of(z * ROWS, ROWS), ROWS)
-                sums[at, :] = jnp.where(active, sums_e[step, at, :], sums[at, :])
-                return carry
-
-            lax.fori_loop(0, depth, level, 0)
-            mean_a[...] = jnp.where(jnp.broadcast_to(active[0:1], (top, LANES)), means_a[step], mean_a[...])
-            return carry
-
-        lax.fori_loop(least - 1, jnp.minimum(most, AHEAD), pick, 0)
-
-    done = jnp.where(least > AHEAD, AHEAD + 1, AHEAD)
-    middle = jnp.maximum(least, done)
-    scale = jnp.where(least > AHEAD, jnp.float32(10.0 ** (AHEAD + 1)), jnp.float32(10.0**AHEAD))
-    scale = lax.fori_loop(done, middle, plain, scale)
-    lax.fori_loop(middle, most, masked, scale)
+        substep(early, sums_e.at[0], means_a.at[0], 10.0, counts > 1)
 
     shrink = jnp.ones((ROWS, LANES), jnp.float32)
     for step in range(12):
         shrink = jnp.where(counts > step, shrink * 0.1, shrink)
+    shrink_0 = (2.0 / 3.0) * shrink
+    copies = [
+        pltpu.make_async_copy(state.at[:, lo:hi], new_ref.at[:, lo:hi], out_sems.at[i]) for i, (lo, hi) in enumerate(bounds)
+    ]
+
+    def finish(z, e):
+        add_0 = jnp.broadcast_to(add[z : z + 1, :], (ROWS, LANES))
+        add_a = jnp.broadcast_to(mean_a[z : z + 1, :], (ROWS, LANES))
+        new_0, new_1 = [], []
+        for k in range(parts):
+            a = state[0, z, k * ROWS : (k + 1) * ROWS, :]
+            u0 = (a - e[k]) * shrink_0 + add_0
+            new_0.append(u0)
+            new_1.append((a * shrink + add_a) - u0)
+        for k in range(parts):
+            state[0, z, pl.ds(k, ROWS, stride=parts), :] = new_0[k]
+            state[1, z, pl.ds(k, ROWS, stride=parts), :] = new_1[k]
+        for (_, hi), copy in zip(bounds, copies):
+            if hi == z + 1:
+                copy.start()
+
+    def set_add():
+        add[...] = (2.0 / 3.0) * (mean_a[...] - saturation)
+
+    done = jnp.where(least > AHEAD, AHEAD + 1, 2)
+
+    @pl.when(most > done)
+    def _():
+        scale = jnp.where(least > AHEAD, jnp.float32(10.0 ** (AHEAD + 1)), jnp.float32(100.0))
+        middle = jnp.minimum(jnp.maximum(least, done), most - 1)
+        scale = lax.fori_loop(done, middle, plain, scale)
+        scale = lax.fori_loop(middle, most - 1, masked, scale)
+        active = counts > most - 1
+        pieces = advance(scale, sums, profiles, bias, padded, padded_a, mean_a, mean_a, width, depth, active)
+        sweep(state, state, 0, active, None, None, False, pieces + [set_add])
+        sweep(state, state, 1, active, bias, sums, True, (), finish)
+
+    @pl.when(most <= done)
+    def _():
+        set_add()
+        for z in range(depth):
+            finish(z, [state[1, z, k * ROWS : (k + 1) * ROWS, :] for k in range(parts)])
+
     new_a = mean_a[...]
     new_e = mean_of(sums, width) * shrink[0:1] + saturation
     old_a = profiles[0]
@@ -492,37 +512,13 @@
     tend_1 = (new_a - old_a) - tend_0
     tend_ref[:, 0, :] = tend_0[0:depth]
     tend_ref[:, 1, :] = tend_1[0:depth]
-    bias[...] = (2.0 / 3.0) * (new_a - saturation)
-    shrink_0 = (2.0 / 3.0) * shrink
-
-    def finish(z):
-        add_0 = jnp.broadcast_to(bias[pl.ds(z, 1), :], (ROWS, LANES))
-        add_a = jnp.broadcast_to(mean_a[pl.ds(z, 1), :], (ROWS, LANES))
-        new_0, new_1 = [], []
-        for k in range(parts):
-            a = state[0, z, k * ROWS : (k + 1) * ROWS, :]
-            e = state[1, z, k * ROWS : (k + 1) * ROWS, :]
-            u0 = (a - e) * shrink_0 + add_0
-            new_0.append(u0)
-            new_1.append((a * shrink + add_a) - u0)
-        for k in range(parts):
-            state[0, z, pl.ds(k, ROWS, stride=parts), :] = new_0[k]
-            state[1, z, pl.ds(k, ROWS, stride=parts), :] = new_1[k]
-
-    stores = []
-    for i, (lo, hi) in enumerate(bounds):
-        for z in range(lo, hi):
-            finish(z)
-        copy = pltpu.make_async_copy(state.at[:, lo:hi], new_ref.at[:, lo:hi], out_sems.at[i])
-        copy.start()
-        stores.append(copy)
-    for copy in stores:
+    for copy in copies:
         copy.wait()
     dsum_copy.wait()
 
 
-def rest(history, dsum, counts, sums_e, means_a, profiles):
-    _, fields, depth, width, _ = history.shape
+def rest(early, ahead, dsum, counts, sums_e, means_a, profiles):
+    fields, depth, width, _ = early.shape
     top = profiles.shape[1]
     vmem = pl.BlockSpec(memory_space=pltpu.VMEM)
     hbm = pl.BlockSpec(memory_space=pltpu.HBM)
@@ -532,15 +528,16 @@
         out_shape=(
             jax.ShapeDtypeStruct(dsum.shape, jnp.float32),
             jax.ShapeDtypeStruct((depth, fields, LANES), jnp.float32),
-            jax.ShapeDtypeStruct(history.shape[1:], jnp.float32),
+            jax.ShapeDtypeStruct(early.shape, jnp.float32),
         ),
-        in_specs=[vmem] * 6,
+        in_specs=[vmem] * 7,
         out_specs=(hbm, vmem, hbm),
         scratch_shapes=[
-            pltpu.VMEM(history.shape[1:], jnp.float32),
+            pltpu.VMEM(early.shape, jnp.float32),
             pltpu.VMEM(sums_e.shape[1:], jnp.float32),
             padded,
             padded,
+            pltpu.VMEM((top, LANES), jnp.float32),
             pltpu.VMEM((top, LANES), jnp.float32),
             pltpu.VMEM((top, LANES), jnp.float32),
             pltpu.SemaphoreType.DMA((CHUNKS,)),
@@ -548,7 +545,7 @@
         ],
         compiler_params=pltpu.CompilerParams(vmem_limit_bytes=8 * 2**20),
         name="rest",
-    )(history, dsum, counts, sums_e, means_a, profiles)
+    )(early, ahead, dsum, counts, sums_e, means_a, profiles)
 
 
 def on_device(dynamics, adjacency, cloud_state, span_source, substeps):

time: 26.5 us -> 25.5 us (0.962)
  Pallas kernels: 25.7 us -> 24.7 us
    pallas_call x1, Pallas kernels: 21.6 us -> 20.8 us  [first(): pl.pallas_call(functools.partial(first_kernel, devices, span, cut(depth))...]
where the time goes in v5:
time: 25.5 us; the launch traced here: 25.3 us
  Pallas kernels  24.7 us (97%)
  between operations  0.64 us (3%)
    pallas_call x1, Pallas kernels, first(): pl.pallas_call(functools.partial(first_kernel, devices, span, cut(depth))...  20.8 us
    pallas_call x1, Pallas kernels, rest(): pl.pallas_call(functools.partial(rest_kernel, cut(depth)), out_shape=(jax...  3.94 us

profile of v5, /device:TPU:0, one launch (start us, length us, event | category | flops | bytes accessed | tf_op | source)
XLA Modules:
  0.0 25.3 jit_solution(10034340104483154756)
XLA Ops:
  0.6 20.8 %first.1 = (f32[2,58,64,128]{3,2,1,0:T(8,128)S(1)}, f32[2,58,64,128]{3,2,1,0:T(8,128)S(1)}, f32[2,72,512]{2,1,0:T(8,128)S(1)}, s32[8,128]{1,0:T(8,128)S(1)}, f32...) custom-call(f32[2,72,512]{2,1,0:T(8,128)} %dyn_hbm.1, s32[2,128]{1,0:T(2,128)} %adj_hbm.1, ...), custom_call_target="tpu_custom_call" | custom-call | tf_op jit(solution)/shard_map/first/pallas_call | solution.py:380
  21.4 3.9 %rest.1 = (f32[2,72,512]{2,1,0:T(8,128)}, f32[58,2,128]{2,1,0:T(2,128)}, f32[2,58,64,128]{3,2,1,0:T(8,128)}) custom-call(f32[2,58,64,128]{3,2,1,0:T(8,128)S(1)} %get-tuple-element.13.early, f32[2,58,64,128]{3,2,1,0:T(8,128)S(1)} %get-tuple-element.14.ahead, f32[2,72,512]{2,1,0:T(8,128)S(1)} %get-tuple-element.15.dsum_ref, ...), custom_call_target="tpu_custom_call" | custom-call | tf_op jit(solution)/shard_map/rest/pallas_call | solution.py:526

commit v6 on v5

--- a/solution.py
+++ b/solution.py
@@ -12,6 +12,7 @@
 PAD = 8
 CHUNKS = 6
 AHEAD = 7
+EARLY_CHUNKS = 2
 
 
 def odious(node):
@@ -251,23 +252,6 @@
     message = lax.dot_general(to_device, to_lane, (((1,), (1,)), ((), ())), preferred_element_type=jnp.float32)
     outgoing[...] = message.astype(jnp.int32).reshape(outgoing.shape)
 
-    pl.semaphore_wait(barrier, 2 + 3 + 3 + ROWS - 1)
-
-    def send(src, dst, send_sem, recv_sem, device):
-        copy = pltpu.make_async_remote_copy(
-            src_ref=src, dst_ref=dst, send_sem=send_sem, recv_sem=recv_sem, device_id=(device,), device_id_type=pl.DeviceIdType.MESH
-        )
-        copy.start()
-        return copy
-
-    rows_y = outgoing.shape[0] // 4
-    leg_y, leg_z, leg_x = [], [], []
-    for step in range(1, 4):
-        to, device = along(strides[0], step)
-        leg_y.append(send(outgoing.at[pl.ds(to * rows_y, rows_y)], arrived_y.at[step], leg_send.at[step], leg_recv.at[step], device))
-    up = send(edges, halo.at[0], halo_send.at[0], halo_recv.at[0], above)
-    down = send(edges, halo.at[1], halo_send.at[1], halo_recv.at[1], below)
-
     local[3].wait()
     weights = edge_weights(partner_places(me, devices, adj, nodes // 16, half), half)
     row = lax.broadcasted_iota(jnp.int32, (nodes, LANES), 0)
@@ -293,15 +277,38 @@
         sums[1, pl.ds(at, ROWS), :] = total_of(all_e)
         return carry
 
-    for (lo, hi), copy in zip(bounds, loads):
-        copy.wait()
-        lax.fori_loop(lo, hi, begin, 0, unroll=2)
+    def begin_part(part):
+        for (lo, hi), copy in list(zip(bounds, loads))[part]:
+            copy.wait()
+            lax.fori_loop(lo, hi, begin, 0, unroll=2)
+
+    begin_part(slice(0, EARLY_CHUNKS))
+
+    pl.semaphore_wait(barrier, 2 + 3 + 3 + ROWS - 1)
+
+    def send(src, dst, send_sem, recv_sem, device):
+        copy = pltpu.make_async_remote_copy(
+            src_ref=src, dst_ref=dst, send_sem=send_sem, recv_sem=recv_sem, device_id=(device,), device_id_type=pl.DeviceIdType.MESH
+        )
+        copy.start()
+        return copy
+
+    rows_y = outgoing.shape[0] // 4
+    leg_y, leg_z, leg_x = [], [], []
+    for step in range(1, 4):
+        to, device = along(strides[0], step)
+        leg_y.append(send(outgoing.at[pl.ds(to * rows_y, rows_y)], arrived_y.at[step], leg_send.at[step], leg_recv.at[step], device))
+    up = send(edges, halo.at[0], halo_send.at[0], halo_recv.at[0], above)
+    down = send(edges, halo.at[1], halo_send.at[1], halo_recv.at[1], below)
+
+    begin_part(slice(EARLY_CHUNKS, CHUNKS))
 
     start_a = mean_of(sums.at[0], width)
     start_e = mean_of(sums.at[1], width)
     saturation = saturation_of(top, depth)
     bias_a[...] = -spread(padded, start_a, depth)
     sweep(loaded, early, 0, None, bias_a, None, False)
+    sweep(early, state, 0, None, None, None, False)
 
     for copy in leg_y:
         copy.wait_recv()
@@ -310,6 +317,12 @@
     for step in range(1, 4):
         to, device = along(strides[1], step)
         leg_z.append(send(merged.at[to], arrived_z.at[step], leg_send.at[3 + step], leg_recv.at[3 + step], device))
+
+    def further(step, carry):
+        sweep(state, state, 0, None, None, None, False)
+        return carry
+
+    lax.fori_loop(2, AHEAD, further, 0)
 
     up.wait()
     down.wait()
@@ -333,7 +346,8 @@
         pieces = advance(
             scale, sums_e.at[before], profiles, bias, padded, padded_a, mean_a.at[before], mean_a.at[1], width, depth
         )
-        sweep(source, state, 0, None, None, None, False, pieces)
+        for piece in pieces:
+            piece()
         sweep(source, state, 1, None, bias, sums_e.at[1], True)
         return scale * 10.0
 

time: 25.5 us -> 25.5 us (level)
  the two profiles are of different devices: /device:TPU:0 before, /device:TPU:24 now
where the time goes in v6:
time: 25.5 us; the launch traced here: 25.3 us
  Pallas kernels  24.7 us (97%)
  between operations  0.64 us (3%)
    pallas_call x1, Pallas kernels, first(): pl.pallas_call(functools.partial(first_kernel, devices, span, cut(depth))...  17.5 us
    pallas_call x1, Pallas kernels, rest(): pl.pallas_call(functools.partial(rest_kernel, cut(depth)), out_shape=(jax...  7.2 us

profile of v6, /device:TPU:24, one launch (start us, length us, event | category | flops | bytes accessed | tf_op | source)
XLA Modules:
  0.0 25.3 jit_solution(8353451935777126)
XLA Ops:
  0.6 17.5 %first.1 = (f32[2,58,64,128]{3,2,1,0:T(8,128)S(1)}, f32[2,58,64,128]{3,2,1,0:T(8,128)S(1)}, f32[2,72,512]{2,1,0:T(8,128)S(1)}, s32[8,128]{1,0:T(8,128)S(1)}, f32...) custom-call(f32[2,72,512]{2,1,0:T(8,128)} %dyn_hbm.1, s32[2,128]{1,0:T(2,128)} %adj_hbm.1, ...), custom_call_target="tpu_custom_call" | custom-call | tf_op jit(solution)/shard_map/first/pallas_call | solution.py:394
  18.1 7.2 %rest.1 = (f32[2,72,512]{2,1,0:T(8,128)}, f32[58,2,128]{2,1,0:T(2,128)}, f32[2,58,64,128]{3,2,1,0:T(8,128)}) custom-call(f32[2,58,64,128]{3,2,1,0:T(8,128)S(1)} %get-tuple-element.13.early, f32[2,58,64,128]{3,2,1,0:T(8,128)S(1)} %get-tuple-element.14.ahead, f32[2,72,512]{2,1,0:T(8,128)S(1)} %get-tuple-element.15.dsum_ref, ...), custom_call_target="tpu_custom_call" | custom-call | tf_op jit(solution)/shard_map/rest/pallas_call | solution.py:540

commit v7 on v6

--- a/solution.py
+++ b/solution.py
@@ -11,7 +11,7 @@
 ROWS = 8
 PAD = 8
 CHUNKS = 6
-AHEAD = 7
+AHEAD = 8
 EARLY_CHUNKS = 2
 
 
@@ -213,11 +213,11 @@
     def greet(device):
         pl.semaphore_signal(barrier, inc=1, device_id=(device,), device_id_type=pl.DeviceIdType.MESH)
 
-    greet(above)
-    greet(below)
     for stride in strides:
         for step in range(1, 4):
             greet(along(stride, step)[1])
+    greet(above)
+    greet(below)
     for step in range(1, ROWS):
         greet(me - member + (member + step) % ROWS)
 
@@ -468,7 +468,7 @@
     def _():
         substep(ahead, sums_e.at[1], means_a.at[1], 10.0**AHEAD, None)
 
-    @pl.when(least <= AHEAD)
+    @pl.when((least <= AHEAD) & (most > 2))
     def _():
         substep(early, sums_e.at[0], means_a.at[0], 10.0, counts > 1)
 
@@ -501,18 +501,24 @@
 
     done = jnp.where(least > AHEAD, AHEAD + 1, 2)
 
+    def last_substep(src, source_sums, source_mean, scale, active):
+        pieces = advance(scale, source_sums, profiles, bias, padded, padded_a, source_mean, mean_a, width, depth, active)
+        sweep(src, state, 0, active, None, None, False, pieces + [set_add])
+        sweep(src, state, 1, active, bias, sums, True, (), finish)
+
     @pl.when(most > done)
     def _():
         scale = jnp.where(least > AHEAD, jnp.float32(10.0 ** (AHEAD + 1)), jnp.float32(100.0))
         middle = jnp.minimum(jnp.maximum(least, done), most - 1)
         scale = lax.fori_loop(done, middle, plain, scale)
         scale = lax.fori_loop(middle, most - 1, masked, scale)
-        active = counts > most - 1
-        pieces = advance(scale, sums, profiles, bias, padded, padded_a, mean_a, mean_a, width, depth, active)
-        sweep(state, state, 0, active, None, None, False, pieces + [set_add])
-        sweep(state, state, 1, active, bias, sums, True, (), finish)
-
-    @pl.when(most <= done)
+        last_substep(state, sums, mean_a, scale, counts > most - 1)
+
+    @pl.when(most <= 2)
+    def _():
+        last_substep(early, sums_e.at[0], means_a.at[0], 10.0, counts > 1)
+
+    @pl.when((most <= done) & (most > 2))
     def _():
         set_add()
         for z in range(depth):

time: 25.5 us -> 24.7 us (0.969)
  the two profiles are of different devices: /device:TPU:24 before, /device:TPU:0 now
where the time goes in v7:
time: 24.7 us; the launch traced here: 24.6 us
  Pallas kernels  23.9 us (97%)
  between operations  0.64 us (3%)
    pallas_call x1, Pallas kernels, first(): pl.pallas_call(functools.partial(first_kernel, devices, span, cut(depth))...  20.5 us
    pallas_call x1, Pallas kernels, rest(): pl.pallas_call(functools.partial(rest_kernel, cut(depth)), out_shape=(jax...  3.41 us

profile of v7, /device:TPU:0, one launch (start us, length us, event | category | flops | bytes accessed | tf_op | source)
XLA Modules:
  0.0 24.6 jit_solution(190286900179392340)
XLA Ops:
  0.6 20.5 %first.1 = (f32[2,58,64,128]{3,2,1,0:T(8,128)S(1)}, f32[2,58,64,128]{3,2,1,0:T(8,128)S(1)}, f32[2,72,512]{2,1,0:T(8,128)S(1)}, s32[8,128]{1,0:T(8,128)S(1)}, f32...) custom-call(f32[2,72,512]{2,1,0:T(8,128)} %dyn_hbm.1, s32[2,128]{1,0:T(2,128)} %adj_hbm.1, ...), custom_call_target="tpu_custom_call" | custom-call | tf_op jit(solution)/shard_map/first/pallas_call | solution.py:394
  21.2 3.4 %rest.1 = (f32[2,72,512]{2,1,0:T(8,128)}, f32[58,2,128]{2,1,0:T(2,128)}, f32[2,58,64,128]{3,2,1,0:T(8,128)}) custom-call(f32[2,58,64,128]{3,2,1,0:T(8,128)S(1)} %get-tuple-element.13.early, f32[2,58,64,128]{3,2,1,0:T(8,128)S(1)} %get-tuple-element.14.ahead, f32[2,72,512]{2,1,0:T(8,128)S(1)} %get-tuple-element.15.dsum_ref, ...), custom_call_target="tpu_custom_call" | custom-call | tf_op jit(solution)/shard_map/rest/pallas_call | solution.py:546

commit v8 on v7

--- a/solution.py
+++ b/solution.py
@@ -11,6 +11,7 @@
 ROWS = 8
 PAD = 8
 CHUNKS = 6
+OUT_CHUNKS = 12
 AHEAD = 8
 EARLY_CHUNKS = 2
 
@@ -377,8 +378,8 @@
         copy.wait_send()
 
 
-def cut(depth):
-    cuts = [round(i * depth / CHUNKS) for i in range(CHUNKS + 1)]
+def cut(depth, parts):
+    cuts = [round(i * depth / parts) for i in range(parts + 1)]
     return tuple(zip(cuts[:-1], cuts[1:]))
 
 
@@ -392,7 +393,7 @@
     hbm = pl.BlockSpec(memory_space=pltpu.HBM)
     profile = pltpu.VMEM((top, LANES), jnp.float32)
     return pl.pallas_call(
-        functools.partial(first_kernel, devices, span, cut(depth)),
+        functools.partial(first_kernel, devices, span, cut(depth, CHUNKS)),
         out_shape=(
             jax.ShapeDtypeStruct(cloud_state.shape, jnp.float32),
             jax.ShapeDtypeStruct(cloud_state.shape, jnp.float32),
@@ -544,7 +545,7 @@
     hbm = pl.BlockSpec(memory_space=pltpu.HBM)
     padded = pltpu.VMEM((top + 2 * PAD, LANES), jnp.float32)
     return pl.pallas_call(
-        functools.partial(rest_kernel, cut(depth)),
+        functools.partial(rest_kernel, cut(depth, OUT_CHUNKS)),
         out_shape=(
             jax.ShapeDtypeStruct(dsum.shape, jnp.float32),
             jax.ShapeDtypeStruct((depth, fields, LANES), jnp.float32),
@@ -560,7 +561,7 @@
             pltpu.VMEM((top, LANES), jnp.float32),
             pltpu.VMEM((top, LANES), jnp.float32),
             pltpu.VMEM((top, LANES), jnp.float32),
-            pltpu.SemaphoreType.DMA((CHUNKS,)),
+            pltpu.SemaphoreType.DMA((OUT_CHUNKS,)),
             pltpu.SemaphoreType.DMA,
         ],
         compiler_params=pltpu.CompilerParams(vmem_limit_bytes=8 * 2**20),

time: 24.7 us -> 24.9 us (level); the launches traced: 24.6 us -> 24.5 us
  no operation moved by 1% of the time
where the time goes in v8:
time: 24.9 us; the launch traced here: 24.5 us
  Pallas kernels  23.9 us (96%)
  between operations  0.64 us (3%)
    pallas_call x1, Pallas kernels, first(): pl.pallas_call(functools.partial(first_kernel, devices, span, cut(depth,...  20.5 us
    pallas_call x1, Pallas kernels, rest(): pl.pallas_call(functools.partial(rest_kernel, cut(depth, OUT_CHUNKS)), ou...  3.36 us

profile of v8, /device:TPU:0, one launch (start us, length us, event | category | flops | bytes accessed | tf_op | source)
XLA Modules:
  0.0 24.5 jit_solution(455375993962792645)
XLA Ops:
  0.6 20.5 %first.1 = (f32[2,58,64,128]{3,2,1,0:T(8,128)S(1)}, f32[2,58,64,128]{3,2,1,0:T(8,128)S(1)}, f32[2,72,512]{2,1,0:T(8,128)S(1)}, s32[8,128]{1,0:T(8,128)S(1)}, f32...) custom-call(f32[2,72,512]{2,1,0:T(8,128)} %dyn_hbm.1, s32[2,128]{1,0:T(2,128)} %adj_hbm.1, ...), custom_call_target="tpu_custom_call" | custom-call | tf_op jit(solution)/shard_map/first/pallas_call | solution.py:395
  21.2 3.4 %rest.1 = (f32[2,72,512]{2,1,0:T(8,128)}, f32[58,2,128]{2,1,0:T(2,128)}, f32[2,58,64,128]{3,2,1,0:T(8,128)}) custom-call(f32[2,58,64,128]{3,2,1,0:T(8,128)S(1)} %get-tuple-element.13.early, f32[2,58,64,128]{3,2,1,0:T(8,128)S(1)} %get-tuple-element.14.ahead, f32[2,72,512]{2,1,0:T(8,128)S(1)} %get-tuple-element.15.dsum_ref, ...), custom_call_target="tpu_custom_call" | custom-call | tf_op jit(solution)/shard_map/rest/pallas_call | solution.py:547
